TPU v7x, 128 devices: a whole 4x4x4 slice. The times are simulated.
128 devices in a mesh: row: 8 (over z, core), col: 16 (over y, x).
Axes of the slice: x: 4, y: 4, z: 4, core: 2. Of those that a mesh axis runs over, the one named last changes fastest.
Arguments:
- modes: bfloat16 [384, 65536], P('col', 'row'), may hold values from -6 to 6
- atom_site: int32 [65536, 1], P(('row', 'col')), may hold values from 0 to 15, as said below
- site_owner: int32 [16], replicated, may hold values from 0 to 7, as said below
- translation: int32 [65536], P(('row', 'col')), may hold values from 0 to 12166, as said below
- wavevectors: int32 [4096], P('col'), may hold values from 0 to 12166
Outputs:
- projected: float32 [16, 128, 4096], P('row', None, 'col')
- unfolded: float32 [128, 4096], P('row', 'col')
Inputs may be any that keep to these rules, and one draw needn't show every extreme that they name: `atom_site`: among the atoms of one device (aligned blocks of 512 atoms) no site appears more than 64 times, and some site appears exactly 64 times. `site_owner`: every index of row owns exactly 2 sites. `translation`: the atoms of one site sit on distinct cells.
All inputs are finite; a program needn't handle non-finite values.
Results may differ from a plain program's by a relative error of at most 0.0028.
Values may be sent and summed in bfloat16 or wider, within the bound.
No kernel may reach another device: no remote copies, remote signals or barrier semaphores. Data moves between devices by JAX's collectives and lax.ppermute only.
A program may use at most 128 MiB of HBM per device.

v0:
```python
import math

import jax
import jax.numpy as jnp
from jax import lax
from jax.sharding import PartitionSpec as P

EDGE = 23


def phase_tile(cells, vectors):
    cell_a = cells // (EDGE * EDGE)
    cell_b = cells // EDGE % EDGE
    cell_c = cells % EDGE
    wave_a = vectors // (EDGE * EDGE)
    wave_b = vectors // EDGE % EDGE
    wave_c = vectors % EDGE
    turns = (
        cell_a[:, None] * wave_a[None, :]
        + cell_b[:, None] * wave_b[None, :]
        + cell_c[:, None] * wave_c[None, :]
    ) % EDGE
    angle = turns.astype(jnp.float32) * (2.0 * math.pi / EDGE)
    return jnp.concatenate([jnp.cos(angle), jnp.sin(angle)], axis=1).astype(jnp.bfloat16)


def bucket_slots(site_ids, site_owner, site_dev, capacity):
    count_sites = site_owner.shape[0]
    labels = jnp.arange(count_sites, dtype=jnp.int32)
    onehot = (site_ids[:, None] == labels[None, :]).astype(jnp.int32)
    before = jnp.sum((jnp.cumsum(onehot, axis=0) - onehot) * onehot, axis=1)
    same_owner = site_owner[:, None] == site_owner[None, :]
    earlier = labels[:, None] > labels[None, :]
    within = jnp.sum((same_owner & earlier).astype(jnp.int32), axis=1)
    owners = jnp.sum(onehot * site_owner[None, :], axis=1)
    places = jnp.sum(onehot * within[None, :], axis=1)
    return (owners * site_dev + places) * capacity + before


def body(modes, atom_site, site_owner, translation, wavevectors):
    row_count = lax.axis_size("row")
    col_count = lax.axis_size("col")
    count_sites = site_owner.shape[0]
    site_dev = count_sites // row_count
    local_atoms = atom_site.shape[0]
    capacity = 2 * local_atoms // count_sites
    k_local = wavevectors.shape[0]
    features = lax.all_to_all(modes, "col", split_axis=1, concat_axis=0, tiled=True)
    width = features.shape[0]
    slots = bucket_slots(atom_site[:, 0], site_owner, site_dev, capacity)
    total_slots = row_count * site_dev * capacity
    buffer = jnp.zeros((width, total_slots), jnp.bfloat16).at[:, slots].set(features)
    cell_slots = jnp.zeros((1, total_slots), jnp.int32).at[0, slots].set(translation)
    arrived, arrived_cells = (
        lax.all_to_all(buffer, "row", split_axis=1, concat_axis=1, tiled=True),
        lax.all_to_all(cell_slots, "row", split_axis=1, concat_axis=1, tiled=True),
    )
    rows_piece = lax.all_gather(arrived, "col", axis=1, tiled=True)
    cell_piece = lax.all_gather(arrived_cells, "col", axis=1, tiled=True)
    grouped = rows_piece.reshape(width, -1, site_dev, capacity)
    tiles = phase_tile(cell_piece.reshape(-1), wavevectors)
    tiles = tiles.reshape(grouped.shape[1], site_dev, capacity, 2 * k_local)
    amplitude = jnp.einsum("cfsa,fsak->sck", grouped, tiles, preferred_element_type=jnp.float32)
    power = amplitude[:, :, :k_local] ** 2 + amplitude[:, :, k_local:] ** 2
    norm_value = 3.0 * local_atoms * col_count / site_dev
    projected = jnp.sum(power.reshape(site_dev, 3, width // 3, k_local), axis=1) / norm_value
    unfolded = (
        lax.psum_scatter(jnp.sum(projected, axis=0), "row", scatter_dimension=0, tiled=True)
        / count_sites
    )
    return (projected, unfolded)


def solution(mesh):
    placed = (P("col", "row"), P(("row", "col"), None), P(), P(("row", "col")), P("col"))
    return jax.shard_map(
        body,
        mesh=mesh,
        in_specs=placed,
        out_specs=(P("row", None, "col"), P("row", "col")),
        check_vma=False,
    )
```

profile of v0, /device:TPU:1, one launch (start us, length us, event | category | flops | bytes accessed | tf_op | source)
XLA Modules:
  0.0 206.8 jit_solution(1305287432887754004)
XLA Ops:
  7.2 1.8 copy.27
  8.9 7.6 %all-to-all-start = ((bf16[24,16,512]{2,0,1:T(8,128)(2,1)}), bf16[24,16,512]{2,0,1:T(8,128)(2,1)S(1)}, u32[]{:S(2)}, u32[]{:S(2)}) async-start(bf16[24,16,512]{2,0,1:T(8,128)(2,1)} %bitcast.40), calls=%async_computation | async-start | bytes 786432 | tf_op jit(solution)/shard_map/all_to_all | solution.py:48
  16.6 0.9 convert_reduce_fusion
  17.5 0.7 fusion.19
  18.2 1.1 reduce-window.6
  19.3 0.2 slice_reduce_fusion
  19.6 0.8 select_reduce_fusion.1
  20.4 5.3 %all-to-all-done = bf16[24,16,512]{2,0,1:T(8,128)(2,1)S(1)} async-done(((bf16[24,16,512]{2,0,1:T(8,128)(2,1)}), bf16[24,16,512]{2,0,1:T(8,128)(2,1)S(1)}, u32[]{:S(2)}, u32[]{:S(2)}) %all-to-all-start) | async-done | bytes 393248 | tf_op jit(solution)/shard_map/all_to_all | solution.py:48
  25.7 0.2 copy.22
  25.9 2.6 %scatter_custom_fusion = bf16[384,1024]{0,1:T(8,128)(2,1)S(1)} fusion(s32[512]{0:T(512)S(1)} %bitcast.52, bf16[512,384]{1,0:T(8,128)(2,1)S(1)} %copy.22, bf16[]{:T(256)} %constant.67.clone.1), kind=kCustom, calls=%fused_computation.20 | custom fusion | bytes 786434 | tf_op jit(solution)/shard_map/scatter | solution.py:52
  28.5 19.3 %all_to_all.43 = bf16[384,8,128]{0,2,1:T(8,128)(2,1)} all-to-all(bf16[384,8,128]{0,2,1:T(8,128)(2,1)S(1)} %bitcast.44), channel_id=1, replica_groups=mesh['row'=8,'col'=16] {'row'}, dimensions={1} | all-to-all | bytes 1572864 | tf_op jit(solution)/shard_map/all_to_all | solution.py:55
  47.8 3.2 %scatter_custom_fusion.1 = s32[1024]{0:T(1024)} fusion(s32[512]{0:T(512)S(1)} %bitcast.53, s32[512]{0:T(512)} %param.8, s32[]{:T(128)} %constant.68.clone.1), kind=kCustom, calls=%fused_computation.50 | custom fusion | bytes 4608 | tf_op jit(solution)/shard_map/scatter | solution.py:53
  51.0 4.3 %all-to-all-start.2 = ((s32[1,8,128]{2,0,1:T(1,128)}), s32[1,8,128]{2,0,1:T(1,128)S(1)}, u32[]{:S(2)}, u32[]{:S(2)}) async-start(s32[1,8,128]{2,0,1:T(1,128)} %bitcast.11), calls=%async_computation.2 | async-start | bytes 8192 | tf_op jit(solution)/shard_map/all_to_all | solution.py:56
  55.3 0.7 and_select_fusion.7
  56.0 3.9 %all-to-all-done.2 = s32[1,8,128]{2,0,1:T(1,128)S(1)} async-done(((s32[1,8,128]{2,0,1:T(1,128)}), s32[1,8,128]{2,0,1:T(1,128)S(1)}, u32[]{:S(2)}, u32[]{:S(2)}) %all-to-all-start.2) | async-done | bytes 4128 | tf_op jit(solution)/shard_map/all_to_all | solution.py:56
  59.9 17.3 %all_gather.7 = s32[1,16384]{1,0:T(1,128)S(1)} all-gather(s32[1,1024]{1,0:T(1,128)S(1)} %bitcast.48), channel_id=1, replica_groups=mesh['row'=8,'col'=16] {'col'}, dimensions={1}, use_global_device_ids=true | all-gather | bytes 69632 | tf_op jit(solution)/shard_map/all_gather | solution.py:59
  77.2 0.6 compare_reduce_fusion
  78.0 0.7 divide_reduce_fusion.1
  79.2 0.6 and_select_fusion.1
  79.7 75.2 %cosine_convert_fusion = (bf16[128,2,64,256]{3,2,1,0:T(8,128)(2,1)}, bf16[128,2,64,256]{3,2,1,0:T(8,128)(2,1)}) fusion(s32[256]{0:T(256)S(1)} %get-tuple-element.19, s32[128,2,64]{2,1,0:T(2,128)S(1)} %get-tuple-element.15, s32[256]{0:T(256)S(1)} %get-tuple-element.18, s32[128,2,64]{2,1,0:T(2,128)S(1)} %get-tuple-element.14, s32[256]{0:T(256)S(1)} %get-tuple-element.17, ...), kind=kLoop, calls=%fused_computation.10 | loop fusion | flops 62914560 | bytes 16976896 | tf_op jit(solution)/shard_map/convert
  155.0 12.9 %fusion.9 = f32[2,384,512]{2,1,0:T(8,128)S(1)} fusion(bf16[384,128,2,64]{0,3,2,1:T(8,128)(2,1)} %bitcast.54, bf16[128,2,64,256]{3,2,1,0:T(8,128)(2,1)} %get-tuple-element.13, bf16[128,2,64,256]{3,2,1,0:T(8,128)(2,1)} %get-tuple-element.12), kind=kOutput, calls=%fused_computation.15 | convolution fusion | flops 6476005376 | bytes 30932992 | tf_op jit(solution)/shard_map/cfsa,fsak->sck/dot_general | solution.py:63
  168.1 1.4 fusion.24
  169.5 29.1 %reduce-scatter.2.cloned.1.call-done = f32[16,256]{1,0:T(8,128)} async-done(((f32[128,256]{1,0:T(8,128)}), f32[16,256]{1,0:T(8,128)}) %reduce-scatter.2.cloned.1.call-update) | async-done | bytes 16400 | tf_op jit(solution)/shard_map/reduce_scatter | solution.py:68
  198.6 1.3 broadcast_multiply_fusion.1
  (16 shorter events, 0.9 us)
Async XLA Ops:
  8.9 16.8 %all-to-all-start = ((bf16[24,16,512]{2,0,1:T(8,128)(2,1)}), bf16[24,16,512]{2,0,1:T(8,128)(2,1)S(1)}, u32[]{:S(2)}, u32[]{:S(2)}) async-start(bf16[24,16,512]{2,0,1:T(8,128)(2,1)} %bitcast.40), calls=%async_computation | async-start | bytes 786432 | tf_op jit(solution)/shard_map/all_to_all | solution.py:48
  16.5 138.5 %all-gather.2.cloned.1.call-start = ((), (), s32[]{:S(2)}) async-start(), calls=%async_computation.4 | async-start | bytes 13369344 | tf_op jit(solution)/shard_map/all_gather | solution.py:58
  51.0 8.9 %all-to-all-start.2 = ((s32[1,8,128]{2,0,1:T(1,128)}), s32[1,8,128]{2,0,1:T(1,128)S(1)}, u32[]{:S(2)}, u32[]{:S(2)}) async-start(s32[1,8,128]{2,0,1:T(1,128)} %bitcast.11), calls=%async_computation.2 | async-start | bytes 8192 | tf_op jit(solution)/shard_map/all_to_all | solution.py:56
  55.3 143.4 %reduce-scatter.2.cloned.1.call-start = ((), (), s32[]{:S(2)}) async-start(), calls=%async_computation.5 | async-start | bytes 147456 | tf_op jit(solution)/shard_map/reduce_scatter | solution.py:68
Sparse Core Ops, SparseCore 0:
  48.0 85.8 all-gather.1
  169.6 28.9 reduce-scatter.1
where the time goes:
time: 209 us; the launch traced here: 207 us
  other arithmetic  84.3 us (40%)
  waiting for transfers between devices  38.4 us (18%)
  blocking collectives  36.6 us (18%)
  between operations  14.1 us (7%)
  matrix products  12.9 us (6%)
  starting transfers between devices  11.9 us (6%)
  local copies, waits for them, and re-layouts  8.56 us (4%)
    another operation x3, other arithmetic  76.4 us
    reduce_scatter x1, waiting for transfers between devices, body(): lax.psum_scatter(jnp.sum(projected, axis=0), 'row', scatter_dimension=0,...  29.1 us
    all_to_all x1, blocking collectives, body(): lax.all_to_all(buffer, 'row', split_axis=1, concat_axis=1, tiled=True)  19.3 us
    all_gather x1, blocking collectives, body(): cell_piece = lax.all_gather(arrived_cells, 'col', axis=1, tiled=True)  17.3 us
    dot_general x1, matrix products, body(): jnp.einsum('cfsa,fsak->sck', grouped, tiles, preferred_element_type=jnp.f...  12.9 us
    all_to_all x1, starting transfers between devices, body(): lax.all_to_all(modes, 'col', split_axis=1, concat_axis=0, tiled=True)  7.58 us
    all_to_all x1, waiting for transfers between devices, body(): lax.all_to_all(modes, 'col', split_axis=1, concat_axis=0, tiled=True)  5.3 us
    all_to_all x1, starting transfers between devices, body(): lax.all_to_all(cell_slots, 'row', split_axis=1, concat_axis=1, tiled=True)  4.26 us
  transfers between devices with their start and end apart: 4, of which 3 were waited for; matrix products, arithmetic and copies ran while one was open for 41% of the time, Pallas kernels for 0%

commit v1 on v0

v1 whole, which is shorter than its diff:
```python
import functools
import math

import jax
import jax.numpy as jnp
import numpy as np
from jax import lax
from jax.experimental import pallas as pl
from jax.experimental.pallas import tpu as pltpu
from jax.sharding import PartitionSpec as P

EDGE = 23
HALF = 12
F32, BF16, I32 = jnp.float32, jnp.bfloat16, jnp.int32
CELL_BITS = 14
PANEL = 32
GROUP = 2048
ROWS_LHS = 560
LANES = 384
NT = (((1,), (1,)), ((), ()))


def split_flat(flat):
    first = jnp.floor((flat + 0.5) * (1.0 / (EDGE * EDGE)))
    rest = flat - first * (EDGE * EDGE)
    second = jnp.floor((rest + 0.5) * (1.0 / EDGE))
    return first, second, rest - second * EDGE


def trig_table():
    coord = np.arange(32)
    wave = np.arange(24)
    angle = 2.0 * math.pi * ((wave[:, None] * coord[None, :]) % EDGE) / EDGE
    cos, sin = np.cos(angle), np.sin(angle)
    axes = [
        (0, np.concatenate([cos[:HALF], sin[1:HALF], np.zeros((1, 32))])),
        (24, np.concatenate([cos, sin])),
        (72, np.concatenate([cos[:HALF], sin[:HALF]])),
    ]
    table = np.zeros((96, 192), np.float64)
    for axis, (start, part) in enumerate(axes):
        high = part.astype(jnp.bfloat16).astype(np.float64)
        table[start : start + len(part), axis * 64 : axis * 64 + 32] = high
        table[start : start + len(part), axis * 64 + 32 : axis * 64 + 64] = part - high
    return table.astype(jnp.bfloat16)


def bucket_kernel(owner_ref, modes_ref, meta_ref, out_ref, acc_ref):
    sites = owner_ref.shape[0]
    blocks, block = meta_ref.shape
    owners = sites // 2
    order = []
    for s in range(sites):
        within = jnp.int32(0)
        for earlier in range(s):
            within += (owner_ref[earlier] == owner_ref[s]).astype(I32)
        order.append(owner_ref[s] * 2 + within)
    meta = meta_ref[...]
    site = lax.shift_right_logical(meta, CELL_BITS)
    coords = split_flat((meta & (2**CELL_BITS - 1)).astype(F32))
    hot = [(site == s).astype(F32) for s in range(sites)]
    stacked = jnp.concatenate(hot, axis=0).astype(BF16)
    source = lax.broadcasted_iota(I32, (block, block), 0)
    target = lax.broadcasted_iota(I32, (block, block), 1)
    earlier = (source < target).astype(F32).astype(BF16)
    before = jnp.dot(stacked, earlier, preferred_element_type=F32)
    per_group = GROUP // block
    upper = lax.broadcasted_iota(I32, (sites * blocks, sites * blocks), 0)
    lower = lax.broadcasted_iota(I32, (sites * blocks, sites * blocks), 1)
    same = (upper // per_group == lower // per_group) & (lower < upper)
    offsets = jnp.sum(
        jnp.dot(same.astype(F32).astype(BF16), stacked, preferred_element_type=F32), axis=1, keepdims=True
    )
    before = before + offsets
    rank = jnp.zeros(meta.shape, F32)
    place = jnp.zeros(meta.shape, F32)
    for s in range(sites):
        rank += hot[s] * before[s * blocks : (s + 1) * blocks]
        place += hot[s] * order[s].astype(F32)
    slots = GROUP // 8
    slot_iota = lax.broadcasted_iota(I32, (slots, block), 0).astype(F32)
    pad = jnp.zeros((5, block), F32)
    for group in range(blocks // per_group):
        total = None
        for part in range(per_group):
            b = group * per_group + part
            rows = [c[b : b + 1] for c in coords]
            panel = jnp.concatenate([modes_ref[:, b * block : (b + 1) * block].astype(F32), *rows, pad], axis=0)
            place_row = place[b : b + 1]
            left = jnp.concatenate(
                [jnp.where(place_row == p, panel, 0.0).astype(BF16) for p in range(sites)], axis=0
            )
            right = (slot_iota == rank[b : b + 1]).astype(F32).astype(BF16)
            product = lax.dot_general(left, right, NT, preferred_element_type=F32)
            total = product if total is None else total + product
        for p in range(sites):
            piece = total[p * PANEL : (p + 1) * PANEL].astype(BF16)
            out_ref[p % 2, p // 2, :, group * slots : (group + 1) * slots] = piece


def bucket(owner, modes, meta):
    blocks, block = meta.shape
    owners = owner.shape[0] // 2
    slots = blocks * block // 8
    return pl.pallas_call(
        bucket_kernel,
        out_shape=jax.ShapeDtypeStruct((2, owners, PANEL, slots), BF16),
        in_specs=[
            pl.BlockSpec(memory_space=pltpu.SMEM),
            pl.BlockSpec(memory_space=pltpu.VMEM),
            pl.BlockSpec(memory_space=pltpu.VMEM),
        ],
        out_specs=pl.BlockSpec(memory_space=pltpu.VMEM),
        scratch_shapes=[pltpu.VMEM((8, 128), F32)],
        compiler_params=pltpu.CompilerParams(vmem_limit_bytes=48 * 2**20),
        cost_estimate=pl.CostEstimate(flops=4 * 10**9, bytes_accessed=1500000, transcendentals=0),
    )(owner, modes, meta)


def fill(panel_ref, chunk, table, trig_ref, left_ref, right_ref):
    panel = panel_ref[chunk].astype(F32)
    width = panel.shape[1]
    coord = lax.broadcasted_iota(I32, (32, width), 0).astype(F32)
    hot = []
    for axis in range(3):
        one = (coord == panel[24 + axis : 25 + axis]).astype(F32).astype(BF16)
        hot += [one, one]
    trig_ref[...] = jnp.dot(table, jnp.concatenate(hot, axis=0), preferred_element_type=F32)
    values = panel[:24]
    for pair in range(HALF):
        first = values * trig_ref[2 * pair : 2 * pair + 1]
        if pair < HALF - 1:
            second = values * trig_ref[2 * pair + 1 : 2 * pair + 2]
        else:
            second = jnp.zeros((8, width), F32)
        both = jnp.concatenate([first, second], axis=0).astype(BF16)
        left_ref[48 * pair : 48 * pair + both.shape[0]] = both
    cos1, sin1 = trig_ref[24:48], trig_ref[48:72]
    for pair in range(HALF // 2):
        cos_parts, sin_parts = [], []
        for wave in (2 * pair, 2 * pair + 1):
            cos2, sin2 = trig_ref[72 + wave : 73 + wave], trig_ref[84 + wave : 85 + wave]
            cos_parts.append(cos1 * cos2 - sin1 * sin2)
            sin_parts.append(sin1 * cos2 + cos1 * sin2)
        right_ref[48 * pair : 48 * pair + 48] = jnp.concatenate(cos_parts, axis=0).astype(BF16)
        right_ref[LANES + 48 * pair : LANES + 48 * pair + 48] = jnp.concatenate(sin_parts, axis=0).astype(BF16)


def project_kernel(norm, panel_ref, wave_ref, table_ref, out_ref, trig_ref, left0, left1, right0, right1, acc_ref, power_ref):
    lefts, rights = (left0, left1), (right0, right1)
    chunks = panel_ref.shape[0]
    table = table_ref[...]
    for right in rights:
        right[288:LANES] = jnp.zeros((LANES - 288, right.shape[1]), BF16)
        right[LANES + 288 :] = jnp.zeros((LANES - 288, right.shape[1]), BF16)
    for chunk in range(chunks):
        fill(panel_ref, chunk, table, trig_ref, lefts[chunk % 2], rights[chunk % 2])
        product = lax.dot_general(lefts[chunk % 2][...], rights[chunk % 2][...], NT, preferred_element_type=F32)
        if chunk == 0:
            acc_ref[...] = product
        else:
            acc_ref[...] += product
    scale = 1.0 / norm
    for wave in range(HALF):
        cc = acc_ref[24 * wave : 24 * wave + 24, :LANES]
        cs = acc_ref[24 * wave : 24 * wave + 24, LANES:]
        if wave:
            sc = acc_ref[24 * (11 + wave) : 24 * (12 + wave), :LANES]
            ss = acc_ref[24 * (11 + wave) : 24 * (12 + wave), LANES:]
            same = ((cc - ss) ** 2 + (cs + sc) ** 2) * scale
            other = ((cc + ss) ** 2 + (cs - sc) ** 2) * scale
        else:
            same = other = (cc**2 + cs**2) * scale
        power_ref[48 * wave : 48 * wave + 48] = jnp.concatenate([same, other], axis=0).astype(BF16)
    dests, width = wave_ref.shape
    first, second, third = split_flat(wave_ref[...].astype(F32))
    flip0 = first > HALF - 1
    flip2 = third > HALF - 1
    wave0 = jnp.where(flip0, EDGE - first, first)
    wave1 = jnp.where(flip2 & (second > 0), EDGE - second, second)
    wave2 = jnp.where(flip2, EDGE - third, third)
    column = wave2 * 24.0 + wave1
    group = wave0 * 2.0 + (flip0 != flip2).astype(F32)
    row_iota = lax.broadcasted_iota(I32, (LANES, width), 0).astype(F32)
    for dest in range(dests):
        pick = (row_iota == column[dest : dest + 1]).astype(F32).astype(BF16)
        picked = jnp.dot(power_ref[...], pick, preferred_element_type=F32)
        total = jnp.zeros((24, width), F32)
        for g in range(2 * HALF):
            total += jnp.where(group[dest : dest + 1] == g, picked[24 * g : 24 * g + 24], 0.0)
        out_ref[dest] = total.astype(BF16)


def project(panel, waves, norm):
    sources, rows, slots = panel.shape
    table = jnp.asarray(trig_table())
    return pl.pallas_call(
        functools.partial(project_kernel, norm),
        out_shape=jax.ShapeDtypeStruct((waves.shape[0], 24, waves.shape[1]), BF16),
        in_specs=[pl.BlockSpec(memory_space=pltpu.VMEM)] * 3,
        out_specs=pl.BlockSpec(memory_space=pltpu.VMEM),
        scratch_shapes=[
            pltpu.VMEM((96, slots), F32),
            pltpu.VMEM((ROWS_LHS, slots), BF16),
            pltpu.VMEM((ROWS_LHS, slots), BF16),
            pltpu.VMEM((2 * LANES, slots), BF16),
            pltpu.VMEM((2 * LANES, slots), BF16),
            pltpu.VMEM((ROWS_LHS, 2 * LANES), F32),
            pltpu.VMEM((576, LANES), BF16),
        ],
        compiler_params=pltpu.CompilerParams(vmem_limit_bytes=48 * 2**20),
        cost_estimate=pl.CostEstimate(flops=9 * 10**9, bytes_accessed=1000000, transcendentals=0),
    )(panel, waves, table)


def body(modes, atom_site, site_owner, translation, wavevectors):
    col_count = lax.axis_size("col")
    sites = site_owner.shape[0]
    atoms = translation.shape[0]
    norm = 3.0 * atoms * col_count / 2.0
    packed = jnp.concatenate([atom_site[:, 0] * 2**CELL_BITS + translation, wavevectors])
    packed = jnp.broadcast_to(packed[None], (col_count, packed.shape[0]))
    gathered = lax.all_to_all(packed, "col", split_axis=0, concat_axis=0, tiled=True)
    meta, waves = gathered[:, :atoms], gathered[:, atoms:]
    buckets = bucket(site_owner, modes, meta)
    pieces = []
    for place in range(2):
        panel = lax.all_to_all(buckets[place], "row", split_axis=0, concat_axis=0, tiled=True)
        power = project(panel, waves, norm)
        arrived = lax.all_to_all(power, "col", split_axis=0, concat_axis=0, tiled=True)
        pieces.append(jnp.sum(arrived.astype(F32).reshape(3, -1, arrived.shape[2]), axis=0))
    projected = jnp.stack(pieces)
    local = jnp.sum(projected, axis=0).reshape(lax.axis_size("row"), -1, wavevectors.shape[0])
    shares = lax.all_to_all(local, "row", split_axis=0, concat_axis=0, tiled=True)
    return projected, jnp.sum(shares, axis=0) / sites


def solution(mesh):
    placed = (P("col", "row"), P(("row", "col"), None), P(), P(("row", "col")), P("col"))
    return jax.shard_map(
        body,
        mesh=mesh,
        in_specs=placed,
        out_specs=(P("row", None, "col"), P("row", "col")),
        check_vma=False,
    )
```

time: 209 us -> 105 us (0.50)
  other arithmetic: 84.3 us -> 2.77 us
  Pallas kernels: 0 us -> 33.4 us
  blocking collectives: 36.6 us -> 13.9 us
  waiting for transfers between devices: 38.4 us -> 21.2 us
  starting transfers between devices: 11.9 us -> 28.4 us
  between operations: 14.1 us -> 0.7 us
  matrix products: 12.9 us -> 0 us
  local copies, waits for them, and re-layouts: 8.56 us -> 3.43 us
    another operation x3 -> x1, other arithmetic: 76.4 us -> 0.72 us  [body(): projected = jnp.stack(pieces)]
    pallas_call x0 -> x3, Pallas kernels: none -> 33.4 us  [the longest x2 30.1 us: project(): pl.pallas_call(functools.partial(project_kernel, norm), out_shape=jax.Sha...]
    reduce_scatter x1 -> x0, waiting for transfers between devices: 29.1 us -> none  [body(): lax.psum_scatter(jnp.sum(projected, axis=0), 'row', scatter_dimension=0,...]
    all_gather x1 -> x0, blocking collectives: 17.3 us -> none  [body(): cell_piece = lax.all_gather(arrived_cells, 'col', axis=1, tiled=True)]
    all_to_all x2 -> x5, starting transfers between devices: 11.8 us -> 28.4 us  [the longest x2 11.8 us: body(): lax.all_to_all(buckets[place], 'row', split_axis=0, concat_axis=0, tiled=...]
    dot_general x1 -> x0, matrix products: 12.9 us -> none  [body(): jnp.einsum('cfsa,fsak->sck', grouped, tiles, preferred_element_type=jnp.f...]
    all_to_all x2 -> x5, waiting for transfers between devices: 9.21 us -> 21.2 us  [the longest x2 9.48 us: body(): lax.all_to_all(buckets[place], 'row', split_axis=0, concat_axis=0, tiled=...]
    scatter x2 -> x0, local copies, waits for them, and re-layouts: 5.78 us -> none  [the longest x1 3.17 us: body(): jnp.zeros((1, total_slots), jnp.int32).at[0, slots].set(translation)]
  transfers between devices with their start and end apart: 4 -> 5, of which waited for: 3 -> 3; matrix products, arithmetic and copies ran while one was open for 41% -> 1% of each run, Pallas kernels for 0% -> 29%
where the time goes in v1:
time: 105 us; the launch traced here: 104 us
  Pallas kernels  33.4 us (32%)
  starting transfers between devices  28.4 us (27%)
  waiting for transfers between devices  21.2 us (20%)
  blocking collectives  13.9 us (13%)
  local copies, waits for them, and re-layouts  3.43 us (3%)
  other arithmetic  2.77 us (3%)
    pallas_call x2, Pallas kernels, project(): pl.pallas_call(functools.partial(project_kernel, norm), out_shape=jax.Sha...  30.1 us
    all_to_all x1, blocking collectives, body(): lax.all_to_all(packed, 'col', split_axis=0, concat_axis=0, tiled=True)  13.9 us
    all_to_all x2, starting transfers between devices, body(): lax.all_to_all(buckets[place], 'row', split_axis=0, concat_axis=0, tiled=...  11.8 us
    all_to_all x2, starting transfers between devices, body(): lax.all_to_all(power, 'col', split_axis=0, concat_axis=0, tiled=True)  10.1 us
    all_to_all x2, waiting for transfers between devices, body(): lax.all_to_all(buckets[place], 'row', split_axis=0, concat_axis=0, tiled=...  9.48 us
    all_to_all x2, waiting for transfers between devices, body(): lax.all_to_all(power, 'col', split_axis=0, concat_axis=0, tiled=True)  7.16 us
    all_to_all x1, starting transfers between devices, body(): lax.all_to_all(local, 'row', split_axis=0, concat_axis=0, tiled=True)  6.53 us
    all_to_all x1, waiting for transfers between devices, body(): lax.all_to_all(local, 'row', split_axis=0, concat_axis=0, tiled=True)  4.55 us
  transfers between devices with their start and end apart: 5, of which 3 were waited for; matrix products, arithmetic and copies ran while one was open for 1% of the time, Pallas kernels for 29%

profile of v1, /device:TPU:1, one launch (start us, length us, event | category | flops | bytes accessed | tf_op | source)
XLA Modules:
  0.0 103.8 jit_solution(3160723880244879994)
XLA Ops:
  0.6 0.0 copy-start.3
  0.6 0.7 broadcast_multiply_fusion.1
  1.3 0.0 copy-done.3
  1.3 0.7 copy-done.4
  2.1 13.9 %all_to_all.34 = s32[16,1,768]{2,1,0:T(1,128)S(1)} all-to-all(s32[16,1,768]{2,1,0:T(1,128)S(1)} %broadcast_in_dim.2), channel_id=1, replica_groups=mesh['row'=8,'col'=16] {'col'}, dimensions={0} | all-to-all | bytes 98304 | tf_op jit(solution)/shard_map/all_to_all | solution.py:223
  15.9 0.6 copy-done.1
  16.6 1.0 copy-done
  17.6 3.3 %shard_map.86 = bf16[2,8,32,1024]{3,2,1,0:T(8,128)(2,1)S(1)} custom-call(s32[16]{0:T(128)S(1)} %copy-done.1, bf16[24,8192]{1,0:T(8,128)(2,1)S(1)} %copy-done, s32[16,512]{1,0:T(8,128)S(1)} %slice.16.meta_ref), custom_call_target="tpu_custom_call" | custom-call | flops 4000000000 | bytes 1500000 | tf_op jit(solution)/shard_map/pallas_call | solution.py:105
  20.9 1.1 %slice_bitcast_fusion.1 = (bf16[8,32,1024]{2,1,0:T(8,128)(2,1)}, bf16[8,32,1024]{2,1,0:T(8,128)(2,1)}) fusion(bf16[2,8,32,1024]{3,2,1,0:T(8,128)(2,1)S(1)} %shard_map.86), kind=kLoop, calls=%fused_computation.1 | loop fusion | bytes 2097152 | tf_op jit(solution)/shard_map/squeeze | solution.py:228
  22.0 7.4 %all-to-all-start.1 = ((bf16[8,32,1024]{2,1,0:T(8,128)(2,1)}), bf16[8,32,1024]{2,1,0:T(8,128)(2,1)S(1)}, u32[]{:S(2)}, u32[]{:S(2)}) async-start(bf16[8,32,1024]{2,1,0:T(8,128)(2,1)} %get-tuple-element.2), calls=%async_computation.1 | async-start | bytes 1048576 | tf_op jit(solution)/shard_map/all_to_all | solution.py:228
  29.4 9.5 %all-to-all-done.1.panel_ref = bf16[8,32,1024]{2,1,0:T(8,128)(2,1)S(1)} async-done(((bf16[8,32,1024]{2,1,0:T(8,128)(2,1)}), bf16[8,32,1024]{2,1,0:T(8,128)(2,1)S(1)}, u32[]{:S(2)}, u32[]{:S(2)}) %all-to-all-start.1) | async-done | bytes 524320 | tf_op jit(solution)/shard_map/all_to_all | solution.py:228
  38.9 4.4 %all-to-all-start.3 = ((bf16[8,32,1024]{2,1,0:T(8,128)(2,1)}), bf16[8,32,1024]{2,1,0:T(8,128)(2,1)S(1)}, u32[]{:S(2)}, u32[]{:S(2)}) async-start(bf16[8,32,1024]{2,1,0:T(8,128)(2,1)} %get-tuple-element.3), calls=%async_computation.3 | async-start | bytes 1048576 | tf_op jit(solution)/shard_map/all_to_all | solution.py:228
  43.3 15.0 %shard_map.87 = bf16[16,24,256]{2,1,0:T(8,128)(2,1)} custom-call(bf16[8,32,1024]{2,1,0:T(8,128)(2,1)S(1)} %all-to-all-done.1.panel_ref, s32[16,256]{1,0:T(8,128)S(1)} %slice.18.wave_ref, bf16[96,192]{1,0:T(8,128)(2,1)S(1)} %copy-done.2), custom_call_target="tpu_custom_call" | custom-call | flops 8999999488 | bytes 1000000 | tf_op jit(solution)/shard_map/pallas_call | solution.py:197
  58.3 0.0 all-to-all-done.3.panel_ref
  58.3 3.7 %all-to-all-start.2 = ((bf16[16,24,256]{2,1,0:T(8,128)(2,1)}), bf16[16,24,256]{2,1,0:T(8,128)(2,1)S(1)}, u32[]{:S(2)}, u32[]{:S(2)}) async-start(bf16[16,24,256]{2,1,0:T(8,128)(2,1)} %shard_map.87), calls=%async_computation.2 | async-start | bytes 393216 | tf_op jit(solution)/shard_map/all_to_all | solution.py:230
  62.1 15.0 %shard_map.88 = bf16[16,24,256]{2,1,0:T(8,128)(2,1)} custom-call(bf16[8,32,1024]{2,1,0:T(8,128)(2,1)S(1)} %all-to-all-done.3.panel_ref, s32[16,256]{1,0:T(8,128)S(1)} %slice.18.wave_ref, bf16[96,192]{1,0:T(8,128)(2,1)S(1)} %copy-done.2), custom_call_target="tpu_custom_call" | custom-call | flops 8999999488 | bytes 1000000 | tf_op jit(solution)/shard_map/pallas_call | solution.py:197
  77.1 0.0 all-to-all-done.2
  77.1 6.4 %all-to-all-start.4 = ((bf16[16,24,256]{2,1,0:T(8,128)(2,1)}), bf16[16,24,256]{2,1,0:T(8,128)(2,1)S(1)}, u32[]{:S(2)}, u32[]{:S(2)}) async-start(bf16[16,24,256]{2,1,0:T(8,128)(2,1)} %shard_map.88), calls=%async_computation.4 | async-start | bytes 393216 | tf_op jit(solution)/shard_map/all_to_all | solution.py:230
  83.5 7.2 %all-to-all-done.4 = bf16[16,24,256]{2,1,0:T(8,128)(2,1)S(1)} async-done(((bf16[16,24,256]{2,1,0:T(8,128)(2,1)}), bf16[16,24,256]{2,1,0:T(8,128)(2,1)S(1)}, u32[]{:S(2)}, u32[]{:S(2)}) %all-to-all-start.4) | async-done | bytes 196640 | tf_op jit(solution)/shard_map/all_to_all | solution.py:230
  90.7 0.7 reduce_sum.39
  91.4 6.5 %all-to-all-start.5 = ((f32[8,16,256]{2,1,0:T(8,128)}), f32[8,16,256]{2,1,0:T(8,128)S(1)}, u32[]{:S(2)}, u32[]{:S(2)}) async-start(f32[8,16,256]{2,1,0:T(8,128)} %bitcast.7), calls=%async_computation.5 | async-start | bytes 262144 | tf_op jit(solution)/shard_map/all_to_all | solution.py:234
  97.9 0.7 pad_maximum_fusion
  98.6 4.6 %all-to-all-done.5 = f32[8,16,256]{2,1,0:T(8,128)S(1)} async-done(((f32[8,16,256]{2,1,0:T(8,128)}), f32[8,16,256]{2,1,0:T(8,128)S(1)}, u32[]{:S(2)}, u32[]{:S(2)}) %all-to-all-start.5) | async-done | bytes 131104 | tf_op jit(solution)/shard_map/all_to_all | solution.py:234
  103.2 0.6 broadcast_multiply_fusion
  (14 shorter events, 0.1 us)
Async XLA Ops:
  0.6 0.7 copy-start.3
  1.3 0.7 copy-start.4
  15.9 0.7 copy-start.1
  16.6 1.0 copy-start
  22.0 16.9 %all-to-all-start.1 = ((bf16[8,32,1024]{2,1,0:T(8,128)(2,1)}), bf16[8,32,1024]{2,1,0:T(8,128)(2,1)S(1)}, u32[]{:S(2)}, u32[]{:S(2)}) async-start(bf16[8,32,1024]{2,1,0:T(8,128)(2,1)} %get-tuple-element.2), calls=%async_computation.1 | async-start | bytes 1048576 | tf_op jit(solution)/shard_map/all_to_all | solution.py:228
  38.9 4.4 %copy-start.2 = (bf16[96,192]{1,0:T(8,128)(2,1)S(1)}, bf16[96,192]{1,0:T(8,128)(2,1)}, u32[]{:S(2)}) copy-start(bf16[96,192]{1,0:T(8,128)(2,1)} %constant.9.clone.table_ref) | copy-start | bytes 110596
  38.9 19.4 %all-to-all-start.3 = ((bf16[8,32,1024]{2,1,0:T(8,128)(2,1)}), bf16[8,32,1024]{2,1,0:T(8,128)(2,1)S(1)}, u32[]{:S(2)}, u32[]{:S(2)}) async-start(bf16[8,32,1024]{2,1,0:T(8,128)(2,1)} %get-tuple-element.3), calls=%async_computation.3 | async-start | bytes 1048576 | tf_op jit(solution)/shard_map/all_to_all | solution.py:228
  58.3 18.8 %all-to-all-start.2 = ((bf16[16,24,256]{2,1,0:T(8,128)(2,1)}), bf16[16,24,256]{2,1,0:T(8,128)(2,1)S(1)}, u32[]{:S(2)}, u32[]{:S(2)}) async-start(bf16[16,24,256]{2,1,0:T(8,128)(2,1)} %shard_map.87), calls=%async_computation.2 | async-start | bytes 393216 | tf_op jit(solution)/shard_map/all_to_all | solution.py:230
  77.1 13.6 %all-to-all-start.4 = ((bf16[16,24,256]{2,1,0:T(8,128)(2,1)}), bf16[16,24,256]{2,1,0:T(8,128)(2,1)S(1)}, u32[]{:S(2)}, u32[]{:S(2)}) async-start(bf16[16,24,256]{2,1,0:T(8,128)(2,1)} %shard_map.88), calls=%async_computation.4 | async-start | bytes 393216 | tf_op jit(solution)/shard_map/all_to_all | solution.py:230
  91.4 11.8 %all-to-all-start.5 = ((f32[8,16,256]{2,1,0:T(8,128)}), f32[8,16,256]{2,1,0:T(8,128)S(1)}, u32[]{:S(2)}, u32[]{:S(2)}) async-start(f32[8,16,256]{2,1,0:T(8,128)} %bitcast.7), calls=%async_computation.5 | async-start | bytes 262144 | tf_op jit(solution)/shard_map/all_to_all | solution.py:234

commit v2 on v1

v2 whole, which is shorter than its diff:
```python
import functools
import math

import jax
import jax.numpy as jnp
import numpy as np
from jax import lax
from jax.experimental import pallas as pl
from jax.experimental.pallas import tpu as pltpu
from jax.sharding import PartitionSpec as P

EDGE = 23
HALF = 12
F32, BF16, I32 = jnp.float32, jnp.bfloat16, jnp.int32
CELL_BITS = 14
PANEL = 32
GROUP = 2048
ROWS_LHS = 560
LANES = 384
NT = (((1,), (1,)), ((), ()))


def split_flat(flat):
    first = jnp.floor((flat + 0.5) * (1.0 / (EDGE * EDGE)))
    rest = flat - first * (EDGE * EDGE)
    second = jnp.floor((rest + 0.5) * (1.0 / EDGE))
    return first, second, rest - second * EDGE


def sine_terms():
    nodes = 0.25 * np.cos(np.pi * (np.arange(400) + 0.5) / 800.0)
    turn = 2.0 * nodes
    return [float(c) for c in np.polyfit(turn**2, np.sin(2.0 * np.pi * turn) / turn, 6)]


SINE = sine_terms()


def sine(turn):
    square = turn * turn
    total = SINE[0]
    for term in SINE[1:]:
        total = total * square + term
    return total * turn


def bucket_kernel(owner_ref, modes_ref, meta_ref, out_ref):
    sites = owner_ref.shape[0]
    blocks, block = meta_ref.shape
    order = []
    for s in range(sites):
        within = jnp.int32(0)
        for earlier in range(s):
            within += (owner_ref[earlier] == owner_ref[s]).astype(I32)
        order.append(owner_ref[s] * 2 + within)
    meta = meta_ref[...]
    site = lax.shift_right_logical(meta, CELL_BITS)
    coords = split_flat((meta & (2**CELL_BITS - 1)).astype(F32))
    hot = [(site == s).astype(F32) for s in range(sites)]
    stacked = jnp.concatenate(hot, axis=0).astype(BF16)
    source = lax.broadcasted_iota(I32, (block, block), 0)
    target = lax.broadcasted_iota(I32, (block, block), 1)
    earlier = (source < target).astype(F32).astype(BF16)
    before = jnp.dot(stacked, earlier, preferred_element_type=F32)
    per_group = GROUP // block
    upper = lax.broadcasted_iota(I32, (sites * blocks, sites * blocks), 0)
    lower = lax.broadcasted_iota(I32, (sites * blocks, sites * blocks), 1)
    same = (upper // per_group == lower // per_group) & (lower < upper)
    offsets = jnp.sum(
        jnp.dot(same.astype(F32).astype(BF16), stacked, preferred_element_type=F32), axis=1, keepdims=True
    )
    before = before + offsets
    rank = jnp.zeros(meta.shape, F32)
    place = jnp.zeros(meta.shape, F32)
    for s in range(sites):
        rank += hot[s] * before[s * blocks : (s + 1) * blocks]
        place += hot[s] * order[s].astype(F32)
    slots = GROUP // 8
    slot_iota = lax.broadcasted_iota(I32, (slots, block), 0).astype(F32)
    pad = jnp.zeros((5, block), F32)
    for group in range(blocks // per_group):
        total = None
        for part in range(per_group):
            b = group * per_group + part
            rows = [c[b : b + 1] for c in coords]
            panel = jnp.concatenate([modes_ref[:, b * block : (b + 1) * block].astype(F32), *rows, pad], axis=0)
            place_row = place[b : b + 1]
            left = jnp.concatenate(
                [jnp.where(place_row == p, panel, 0.0).astype(BF16) for p in range(sites)], axis=0
            )
            right = (slot_iota == rank[b : b + 1]).astype(F32).astype(BF16)
            product = lax.dot_general(left, right, NT, preferred_element_type=F32)
            total = product if total is None else total + product
        for p in range(sites):
            piece = total[p * PANEL : (p + 1) * PANEL].astype(BF16)
            out_ref[p // 2, p % 2, :, group * slots : (group + 1) * slots] = piece


def bucket(owner, modes, meta):
    blocks, block = meta.shape
    owners = owner.shape[0] // 2
    slots = blocks * block // 8
    return pl.pallas_call(
        bucket_kernel,
        out_shape=jax.ShapeDtypeStruct((owners, 2, PANEL, slots), BF16),
        in_specs=[
            pl.BlockSpec(memory_space=pltpu.SMEM),
            pl.BlockSpec(memory_space=pltpu.VMEM),
            pl.BlockSpec(memory_space=pltpu.VMEM),
        ],
        out_specs=pl.BlockSpec(memory_space=pltpu.VMEM),
        compiler_params=pltpu.CompilerParams(vmem_limit_bytes=48 * 2**20),
        cost_estimate=pl.CostEstimate(flops=4 * 10**9, bytes_accessed=1500000, transcendentals=0),
    )(owner, modes, meta)


def fill_steps(panel_ref, trig_ref, left_ref, right_ref):
    width = panel_ref.shape[1]

    def lookup():
        cells = panel_ref[16:32].astype(F32)
        rows = lax.broadcasted_iota(I32, (24, width), 0).astype(F32)
        waves = [
            (jnp.where(rows < HALF, rows, rows - 11.0), jnp.where(rows < HALF, 0.25, 0.0)),
            (rows, 0.25),
            (rows, 0.0),
            (jnp.where(rows < HALF, rows, rows - 12.0), jnp.where(rows < HALF, 0.25, 0.0)),
        ]
        for part, axis in enumerate((0, 1, 1, 2)):
            wave, shift = waves[part]
            turn = wave * (cells[8 + axis : 9 + axis] * (1.0 / EDGE)) + shift
            trig_ref[24 * part : 24 * part + 24] = sine(turn - jnp.round(turn))

    def left(pair):
        values = panel_ref[...].astype(F32)[:24]
        first = values * trig_ref[2 * pair : 2 * pair + 1]
        if pair < HALF - 1:
            second = values * trig_ref[2 * pair + 1 : 2 * pair + 2]
        else:
            second = jnp.zeros((8, width), F32)
        both = jnp.concatenate([first, second], axis=0).astype(BF16)
        left_ref[48 * pair : 48 * pair + both.shape[0]] = both

    def right(pair):
        cos1, sin1 = trig_ref[24:48], trig_ref[48:72]
        cos_parts, sin_parts = [], []
        for wave in (2 * pair, 2 * pair + 1):
            cos2, sin2 = trig_ref[72 + wave : 73 + wave], trig_ref[84 + wave : 85 + wave]
            cos_parts.append(cos1 * cos2 - sin1 * sin2)
            sin_parts.append(sin1 * cos2 + cos1 * sin2)
        right_ref[48 * pair : 48 * pair + 48] = jnp.concatenate(cos_parts, axis=0).astype(BF16)
        right_ref[LANES + 48 * pair : LANES + 48 * pair + 48] = jnp.concatenate(sin_parts, axis=0).astype(BF16)

    steps = [lookup]
    for pair in range(HALF):
        steps.append(functools.partial(left, pair))
        if pair % 2:
            steps.append(functools.partial(right, pair // 2))
    return steps


def project_kernel(norm, panel_ref, wave_ref, out_ref, trig_ref, left0, left1, right0, right1, acc_ref, power_ref):
    lefts, rights = (left0, left1), (right0, right1)
    sources, places = panel_ref.shape[:2]
    for right in rights:
        right[288:LANES] = jnp.zeros((LANES - 288, right.shape[1]), BF16)
        right[LANES + 288 :] = jnp.zeros((LANES - 288, right.shape[1]), BF16)
    dests, width = wave_ref.shape
    first, second, third = split_flat(wave_ref[...].astype(F32))
    flip0 = first > HALF - 1
    flip2 = third > HALF - 1
    wave0 = jnp.where(flip0, EDGE - first, first)
    wave1 = jnp.where(flip2 & (second > 0), EDGE - second, second)
    wave2 = jnp.where(flip2, EDGE - third, third)
    column = wave2 * 24.0 + wave1
    group = wave0 * 2.0 + (flip0 != flip2).astype(F32)
    row_iota = lax.broadcasted_iota(I32, (LANES, width), 0).astype(F32)
    scale = 1.0 / norm

    def steps_of(chunk):
        slot = chunk % 2
        piece = panel_ref.at[chunk % sources, chunk // sources]
        return fill_steps(piece, trig_ref.at[slot], lefts[slot], rights[slot])

    def square():
        for wave in range(HALF):
            cc = acc_ref[24 * wave : 24 * wave + 24, :LANES]
            cs = acc_ref[24 * wave : 24 * wave + 24, LANES:]
            if wave:
                sc = acc_ref[24 * (11 + wave) : 24 * (12 + wave), :LANES]
                ss = acc_ref[24 * (11 + wave) : 24 * (12 + wave), LANES:]
                same = ((cc - ss) ** 2 + (cs + sc) ** 2) * scale
                other = ((cc + ss) ** 2 + (cs - sc) ** 2) * scale
            else:
                same = other = (cc**2 + cs**2) * scale
            power_ref[48 * wave : 48 * wave + 48] = jnp.concatenate([same, other], axis=0).astype(BF16)

    def pick(dest):
        chosen = (row_iota == column[dest : dest + 1]).astype(F32).astype(BF16)
        return jnp.dot(power_ref[...], chosen, preferred_element_type=F32)

    def store(place, dest, picked):
        total = jnp.zeros((24, width), F32)
        for g in range(2 * HALF):
            total += jnp.where(group[dest : dest + 1] == g, picked[24 * g : 24 * g + 24], 0.0)
        out_ref[dest, place] = total.astype(BF16)

    chunks = places * sources
    for step in steps_of(0):
        step()
    for chunk in range(chunks):
        slot = chunk % 2
        ahead = steps_of(chunk + 1) if chunk + 1 < chunks else []
        product = lax.dot_general(lefts[slot][...], rights[slot][...], NT, preferred_element_type=F32)
        for step in ahead:
            step()
        if chunk % sources == 0:
            acc_ref[...] = product
        else:
            acc_ref[...] += product
        if (chunk + 1) % sources == 0:
            place = chunk // sources
            square()
            picked = pick(0)
            for dest in range(dests):
                following = pick(dest + 1) if dest + 1 < dests else None
                store(place, dest, picked)
                picked = following


def project(panel, waves, norm):
    sources, places, rows, slots = panel.shape
    return pl.pallas_call(
        functools.partial(project_kernel, norm),
        out_shape=jax.ShapeDtypeStruct((waves.shape[0], places, 24, waves.shape[1]), BF16),
        in_specs=[pl.BlockSpec(memory_space=pltpu.VMEM)] * 2,
        out_specs=pl.BlockSpec(memory_space=pltpu.VMEM),
        scratch_shapes=[
            pltpu.VMEM((2, 96, slots), F32),
            pltpu.VMEM((ROWS_LHS, slots), BF16),
            pltpu.VMEM((ROWS_LHS, slots), BF16),
            pltpu.VMEM((2 * LANES, slots), BF16),
            pltpu.VMEM((2 * LANES, slots), BF16),
            pltpu.VMEM((ROWS_LHS, 2 * LANES), F32),
            pltpu.VMEM((576, LANES), BF16),
        ],
        compiler_params=pltpu.CompilerParams(vmem_limit_bytes=48 * 2**20),
        cost_estimate=pl.CostEstimate(flops=18 * 10**9, bytes_accessed=2000000, transcendentals=0),
    )(panel, waves)


def body(modes, atom_site, site_owner, translation, wavevectors):
    col_count = lax.axis_size("col")
    sites = site_owner.shape[0]
    atoms = translation.shape[0]
    norm = 3.0 * atoms * col_count / 2.0
    packed = jnp.concatenate([atom_site[:, 0] * 2**CELL_BITS + translation, wavevectors])
    packed = jnp.broadcast_to(packed[None], (col_count, packed.shape[0]))
    gathered = lax.all_to_all(packed, "col", split_axis=0, concat_axis=0, tiled=True)
    meta, waves = gathered[:, :atoms], gathered[:, atoms:]
    buckets = bucket(site_owner, modes, meta)
    panel = lax.all_to_all(buckets, "row", split_axis=0, concat_axis=0, tiled=True)
    power = project(panel, waves, norm)
    arrived = lax.all_to_all(power, "col", split_axis=0, concat_axis=0, tiled=True)
    arrived = arrived.transpose(1, 0, 2, 3).reshape(2, 3, -1, wavevectors.shape[0])
    projected = jnp.sum(arrived.astype(F32), axis=1)
    local = jnp.sum(projected, axis=0).reshape(lax.axis_size("row"), -1, wavevectors.shape[0])
    shares = lax.all_to_all(local, "row", split_axis=0, concat_axis=0, tiled=True)
    return projected, jnp.sum(shares, axis=0) * (1.0 / sites)


def solution(mesh):
    placed = (P("col", "row"), P(("row", "col"), None), P(), P(("row", "col")), P("col"))
    return jax.shard_map(
        body,
        mesh=mesh,
        in_specs=placed,
        out_specs=(P("row", None, "col"), P("row", "col")),
        check_vma=False,
    )
```

time: 105 us -> 94.6 us (0.901)
  starting transfers between devices: 28.4 us -> 12.7 us
  blocking collectives: 13.9 us -> 25.7 us
  Pallas kernels: 33.4 us -> 30.3 us
  waiting for transfers between devices: 21.2 us -> 19.5 us
    all_to_all x4 -> x1, starting transfers between devices: 21.9 us -> 7.38 us  [body(): lax.all_to_all(buckets, 'row', split_axis=0, concat_axis=0, tiled=True)]
    all_to_all x0 -> x1, blocking collectives: none -> 11.8 us  [body(): lax.all_to_all(power, 'col', split_axis=0, concat_axis=0, tiled=True)]
    pallas_call x2 -> x1, Pallas kernels: 30.1 us -> 25.9 us  [project(): pl.pallas_call(functools.partial(project_kernel, norm), out_shape=jax.Sha...]
    all_to_all x4 -> x1, waiting for transfers between devices: 16.6 us -> 15.1 us  [body(): lax.all_to_all(buckets, 'row', split_axis=0, concat_axis=0, tiled=True)]
    all_to_all x1, starting transfers between devices: 6.53 us -> 5.34 us  [body(): lax.all_to_all(local, 'row', split_axis=0, concat_axis=0, tiled=True)]
    squeeze x1 -> x0, local copies, waits for them, and re-layouts: 1.07 us -> none  [body(): buckets[place]]
    unnamed x11 -> x9, local copies, waits for them, and re-layouts: 2.33 us -> 2.33 us
  transfers between devices with their start and end apart: 5 -> 2, of which waited for: 3 -> 2; matrix products, arithmetic and copies ran while one was open for 1% -> 1% of each run, Pallas kernels for 29% -> 0%
where the time goes in v2:
time: 94.6 us; the launch traced here: 94.1 us
  Pallas kernels  30.3 us (32%)
  blocking collectives  25.7 us (27%)
  waiting for transfers between devices  19.5 us (21%)
  starting transfers between devices  12.7 us (13%)
  other arithmetic  2.88 us (3%)
  local copies, waits for them, and re-layouts  2.41 us (3%)
    pallas_call x1, Pallas kernels, project(): pl.pallas_call(functools.partial(project_kernel, norm), out_shape=jax.Sha...  25.9 us
    all_to_all x1, waiting for transfers between devices, body(): lax.all_to_all(buckets, 'row', split_axis=0, concat_axis=0, tiled=True)  15.1 us
    all_to_all x1, blocking collectives, body(): lax.all_to_all(packed, 'col', split_axis=0, concat_axis=0, tiled=True)  13.9 us
    all_to_all x1, blocking collectives, body(): lax.all_to_all(power, 'col', split_axis=0, concat_axis=0, tiled=True)  11.8 us
    all_to_all x1, starting transfers between devices, body(): lax.all_to_all(buckets, 'row', split_axis=0, concat_axis=0, tiled=True)  7.38 us
    all_to_all x1, starting transfers between devices, body(): lax.all_to_all(local, 'row', split_axis=0, concat_axis=0, tiled=True)  5.34 us
    all_to_all x1, waiting for transfers between devices, body(): lax.all_to_all(local, 'row', split_axis=0, concat_axis=0, tiled=True)  4.39 us
    pallas_call x1, Pallas kernels, bucket(): pl.pallas_call(bucket_kernel, out_shape=jax.ShapeDtypeStruct((owners, 2,...  4.33 us
  transfers between devices with their start and end apart: 2, of which 2 were waited for; matrix products, arithmetic and copies ran while one was open for 1% of the time, Pallas kernels for 0%

profile of v2, /device:TPU:1, one launch (start us, length us, event | category | flops | bytes accessed | tf_op | source)
XLA Modules:
  0.0 94.1 jit_solution(6074428010671744554)
XLA Ops:
  0.6 0.0 copy-start.2
  0.6 0.7 broadcast_multiply_fusion.1
  1.3 0.0 copy-done.2
  1.3 0.0 copy-start.3
  1.3 0.7 copy-done.3
  2.1 13.9 %all_to_all.24 = s32[16,1,768]{2,1,0:T(1,128)S(1)} all-to-all(s32[16,1,768]{2,1,0:T(1,128)S(1)} %broadcast_in_dim.2), channel_id=1, replica_groups=mesh['row'=8,'col'=16] {'col'}, dimensions={0} | all-to-all | bytes 98304 | tf_op jit(solution)/shard_map/all_to_all | solution.py:259
  15.9 0.0 copy-start.1
  15.9 0.6 copy-done.1
  16.6 0.0 copy-start
  16.6 1.0 %copy-done = bf16[24,8192]{1,0:T(8,128)(2,1)S(1)} copy-done((bf16[24,8192]{1,0:T(8,128)(2,1)S(1)}, bf16[24,8192]{1,0:T(8,128)(2,1)}, u32[]{:S(2)}) %copy-start) | copy-done | bytes 393240
  17.6 4.3 %shard_map.68 = bf16[8,2,32,1024]{3,2,1,0:T(8,128)(2,1)} custom-call(s32[16]{0:T(128)S(1)} %copy-done.1, bf16[24,8192]{1,0:T(8,128)(2,1)S(1)} %copy-done, s32[16,512]{1,0:T(8,128)S(1)} %slice.8.meta_ref), custom_call_target="tpu_custom_call" | custom-call | flops 4000000000 | bytes 1500000 | tf_op jit(solution)/shard_map/pallas_call | solution.py:103
  21.9 7.4 %all-to-all-start.1 = ((bf16[8,2,32,1024]{3,2,1,0:T(8,128)(2,1)}), bf16[8,2,32,1024]{3,2,1,0:T(8,128)(2,1)S(1)}, u32[]{:S(2)}, u32[]{:S(2)}) async-start(bf16[8,2,32,1024]{3,2,1,0:T(8,128)(2,1)} %shard_map.68), calls=%async_computation.1 | async-start | bytes 2097152 | tf_op jit(solution)/shard_map/all_to_all | solution.py:262
  29.3 15.1 %all-to-all-done.1.panel_ref = bf16[8,2,32,1024]{3,2,1,0:T(8,128)(2,1)S(1)} async-done(((bf16[8,2,32,1024]{3,2,1,0:T(8,128)(2,1)}), bf16[8,2,32,1024]{3,2,1,0:T(8,128)(2,1)S(1)}, u32[]{:S(2)}, u32[]{:S(2)}) %all-to-all-start.1) | async-done | bytes 1048608 | tf_op jit(solution)/shard_map/all_to_all | solution.py:262
  44.4 25.9 %shard_map.69 = bf16[16,2,24,256]{3,2,1,0:T(8,128)(2,1)S(1)} custom-call(bf16[8,2,32,1024]{3,2,1,0:T(8,128)(2,1)S(1)} %all-to-all-done.1.panel_ref, s32[16,256]{1,0:T(8,128)S(1)} %slice.9.wave_ref), custom_call_target="tpu_custom_call" | custom-call | flops 17999998976 | bytes 2000000 | tf_op jit(solution)/shard_map/pallas_call | solution.py:233
  70.3 11.8 %all_to_all.25 = bf16[16,2,24,256]{3,2,1,0:T(8,128)(2,1)S(1)} all-to-all(bf16[16,2,24,256]{3,2,1,0:T(8,128)(2,1)S(1)} %shard_map.69), channel_id=1, replica_groups=mesh['row'=8,'col'=16] {'col'}, dimensions={0} | all-to-all | bytes 786432 | tf_op jit(solution)/shard_map/all_to_all | solution.py:264
  82.1 0.1 convert_reduce_fusion
  82.2 0.7 reduce_sum.37
  82.9 5.3 %all-to-all-start.3 = ((f32[8,16,256]{2,1,0:T(8,128)}), f32[8,16,256]{2,1,0:T(8,128)S(1)}, u32[]{:S(2)}, u32[]{:S(2)}) async-start(f32[8,16,256]{2,1,0:T(8,128)} %bitcast.4), calls=%async_computation.3 | async-start | bytes 262144 | tf_op jit(solution)/shard_map/all_to_all | solution.py:268
  88.2 0.1 convert_bitcast_fusion
  88.3 0.1 copy.9
  88.4 0.8 reduce_sum.34
  89.1 4.4 %all-to-all-done.3 = f32[8,16,256]{2,1,0:T(8,128)S(1)} async-done(((f32[8,16,256]{2,1,0:T(8,128)}), f32[8,16,256]{2,1,0:T(8,128)S(1)}, u32[]{:S(2)}, u32[]{:S(2)}) %all-to-all-start.3) | async-done | bytes 131104 | tf_op jit(solution)/shard_map/all_to_all | solution.py:268
  93.5 0.6 broadcast_multiply_fusion
  (7 shorter events, 0.1 us)
Async XLA Ops:
  0.6 0.7 copy-start.2
  1.3 0.7 copy-start.3
  15.9 0.7 copy-start.1
  16.6 1.0 %copy-start = (bf16[24,8192]{1,0:T(8,128)(2,1)S(1)}, bf16[24,8192]{1,0:T(8,128)(2,1)}, u32[]{:S(2)}) copy-start(bf16[24,8192]{1,0:T(8,128)(2,1)} %modes_ref.1) | copy-start | bytes 1179652
  21.9 22.5 %all-to-all-start.1 = ((bf16[8,2,32,1024]{3,2,1,0:T(8,128)(2,1)}), bf16[8,2,32,1024]{3,2,1,0:T(8,128)(2,1)S(1)}, u32[]{:S(2)}, u32[]{:S(2)}) async-start(bf16[8,2,32,1024]{3,2,1,0:T(8,128)(2,1)} %shard_map.68), calls=%async_computation.1 | async-start | bytes 2097152 | tf_op jit(solution)/shard_map/all_to_all | solution.py:262
  82.9 10.6 %all-to-all-start.3 = ((f32[8,16,256]{2,1,0:T(8,128)}), f32[8,16,256]{2,1,0:T(8,128)S(1)}, u32[]{:S(2)}, u32[]{:S(2)}) async-start(f32[8,16,256]{2,1,0:T(8,128)} %bitcast.4), calls=%async_computation.3 | async-start | bytes 262144 | tf_op jit(solution)/shard_map/all_to_all | solution.py:268

commit v3 on v2

v3 whole, which is shorter than its diff:
```python
import functools
import math

import jax
import jax.numpy as jnp
import numpy as np
from jax import lax
from jax.experimental import pallas as pl
from jax.experimental.pallas import tpu as pltpu
from jax.sharding import PartitionSpec as P

EDGE = 23
HALF = 12
F32, BF16, I32 = jnp.float32, jnp.bfloat16, jnp.int32
CELL_BITS = 14
PANEL = 32
SLOTS = 1024
STRIDE = 3 * SLOTS + 3 * SLOTS // 8
GROUP = 2048
ROWS_LHS = 560
MAIN = 256
SIDE = 48
SIDE_GROUPS = 10
COARSE = (0, 5, 16, 10, 21)
FINE = (0, 1, 12, 2, 13)
ORDER = COARSE + tuple(row for row in range(EDGE) if row not in COARSE)
NT = (((1,), (1,)), ((), ()))


def split_flat(flat):
    first = jnp.floor((flat + 0.5) * (1.0 / (EDGE * EDGE)))
    rest = flat - first * (EDGE * EDGE)
    second = jnp.floor((rest + 0.5) * (1.0 / EDGE))
    return first, second, rest - second * EDGE


def sine_terms():
    nodes = 0.25 * np.cos(np.pi * (np.arange(400) + 0.5) / 800.0)
    turn = 2.0 * nodes
    return [float(c) for c in np.polyfit(turn**2, np.sin(2.0 * np.pi * turn) / turn, 6)]


SINE = sine_terms()


def sine(turn):
    square = turn * turn
    total = SINE[0]
    for term in SINE[1:]:
        total = total * square + term
    return total * turn


def bucket_kernel(sites, block, modes_hbm, meta_ref, out_ref, modes_ref, cell_ref, copied):
    copy = pltpu.make_async_copy(modes_hbm, modes_ref, copied)
    copy.start()
    blocks = meta_ref.shape[0]
    owner_row = meta_ref[0:1, meta_ref.shape[1] - 128 :][:, :sites]
    down = lax.broadcasted_iota(I32, (sites, sites), 0)
    along = lax.broadcasted_iota(I32, (sites, sites), 1)
    owner = jnp.sum(jnp.where(down == along, owner_row, 0), axis=1, keepdims=True)
    same_owner = (owner == owner_row) & (along < down)
    order = (owner * 2 + jnp.sum(same_owner.astype(I32), axis=1, keepdims=True)).astype(F32)
    meta = meta_ref[:, :block]
    site = lax.shift_right_logical(meta, CELL_BITS)
    coords = split_flat((meta & (2**CELL_BITS - 1)).astype(F32))
    hot = [(site == s).astype(F32) for s in range(sites)]
    stacked = jnp.concatenate(hot, axis=0).astype(BF16)
    source = lax.broadcasted_iota(I32, (block, block), 0)
    target = lax.broadcasted_iota(I32, (block, block), 1)
    earlier = (source < target).astype(F32).astype(BF16)
    before = jnp.dot(stacked, earlier, preferred_element_type=F32)
    per_group = GROUP // block
    upper = lax.broadcasted_iota(I32, (sites * blocks, sites * blocks), 0)
    lower = lax.broadcasted_iota(I32, (sites * blocks, sites * blocks), 1)
    same = (upper // per_group == lower // per_group) & (lower < upper)
    offsets = jnp.sum(
        jnp.dot(same.astype(F32).astype(BF16), stacked, preferred_element_type=F32), axis=1, keepdims=True
    )
    before = before + offsets
    rank = jnp.zeros(meta.shape, F32)
    place = jnp.zeros(meta.shape, F32)
    for s in range(sites):
        rank += hot[s] * before[s * blocks : (s + 1) * blocks]
        place += hot[s] * order[s : s + 1]
    copy.wait()
    slots = GROUP // 8
    slot_iota = lax.broadcasted_iota(I32, (slots, block), 0).astype(F32)
    pad = jnp.zeros((5, block), F32)
    for group in range(blocks // per_group):
        total = None
        for part in range(per_group):
            b = group * per_group + part
            rows = [c[b : b + 1] for c in coords]
            panel = jnp.concatenate([modes_ref[:, b * block : (b + 1) * block].astype(F32), *rows, pad], axis=0)
            place_row = place[b : b + 1]
            left = jnp.concatenate(
                [jnp.where(place_row == p, panel, 0.0).astype(BF16) for p in range(sites)], axis=0
            )
            right = (slot_iota == rank[b : b + 1]).astype(F32).astype(BF16)
            product = lax.dot_general(left, right, NT, preferred_element_type=F32)
            total = product if total is None else total + product
        for p in range(sites):
            start = (p % 2) * STRIDE + group * slots
            for part in range(3):
                piece = total[p * PANEL + 8 * part : p * PANEL + 8 * part + 8].astype(BF16)
                out_ref[p // 2, :, start + part * SLOTS : start + part * SLOTS + slots] = piece
            for half in range(slots // 128):
                row = group * (slots // 128) + half
                for axis in range(3):
                    line = total[p * PANEL + 24 + axis : p * PANEL + 25 + axis, 128 * half : 128 * half + 128]
                    cell_ref[p, row : row + 1, 128 * axis : 128 * axis + 128] = line
    for p in range(sites):
        start = (p % 2) * STRIDE + 3 * SLOTS
        out_ref[p // 2, :, start : start + 384] = cell_ref[p].astype(BF16)


def bucket(modes, meta, sites, block):
    rows, atoms = modes.shape
    return pl.pallas_call(
        functools.partial(bucket_kernel, sites, block),
        out_shape=jax.ShapeDtypeStruct((sites // 2, 8, 2 * STRIDE), BF16),
        in_specs=[pl.BlockSpec(memory_space=pl.ANY), pl.BlockSpec(memory_space=pltpu.VMEM)],
        out_specs=pl.BlockSpec(memory_space=pltpu.VMEM),
        scratch_shapes=[
            pltpu.VMEM((rows, atoms), BF16),
            pltpu.VMEM((sites, 8, 384), F32),
            pltpu.SemaphoreType.DMA(()),
        ],
        compiler_params=pltpu.CompilerParams(vmem_limit_bytes=48 * 2**20),
        cost_estimate=pl.CostEstimate(flops=4 * 10**9, bytes_accessed=1500000, transcendentals=0),
    )(modes, meta)


def fill_steps(panel_ref, base, trig_ref, left_ref, right_ref):
    width = SLOTS

    def lookup():
        lines = panel_ref[:, base + 3 * SLOTS : base + STRIDE].astype(F32)
        cells = [
            jnp.concatenate([lines[row : row + 1, 128 * axis : 128 * axis + 128] for row in range(8)], axis=1)
            for axis in range(3)
        ]
        rows = lax.broadcasted_iota(I32, (24, width), 0).astype(F32)
        waves = [
            (jnp.where(rows < HALF, rows, rows - 11.0), jnp.where(rows < HALF, 0.25, 0.0)),
            (rows, 0.25),
            (rows, 0.0),
            (jnp.where(rows < HALF, rows, rows - 12.0), jnp.where(rows < HALF, 0.25, 0.0)),
        ]
        for part, axis in enumerate((0, 1, 1, 2)):
            wave, shift = waves[part]
            turn = wave * (cells[axis] * (1.0 / EDGE)) + shift
            trig_ref[24 * part : 24 * part + 24] = sine(turn - jnp.round(turn))

    def left(pair):
        values = jnp.concatenate(
            [panel_ref[:, base + SLOTS * part : base + SLOTS * part + SLOTS].astype(F32) for part in range(3)], axis=0
        )
        row = ORDER[2 * pair]
        first = values * trig_ref[row : row + 1]
        if pair < HALF - 1:
            row = ORDER[2 * pair + 1]
            second = values * trig_ref[row : row + 1]
        else:
            second = jnp.zeros((8, width), F32)
        both = jnp.concatenate([first, second], axis=0).astype(BF16)
        left_ref[48 * pair : 48 * pair + both.shape[0]] = both

    def plane(wave, low, high):
        cos1, sin1 = trig_ref[24 + low : 24 + high], trig_ref[48 + low : 48 + high]
        cos2, sin2 = trig_ref[72 + wave : 73 + wave], trig_ref[84 + wave : 85 + wave]
        return cos1 * cos2 - sin1 * sin2, sin1 * cos2 + cos1 * sin2

    def right(pair):
        parts = [plane(wave, 0, 24) for wave in (2 * pair + 1, 2 * pair + 2)]
        for part in range(2):
            both = jnp.concatenate([parts[0][part], parts[1][part]], axis=0).astype(BF16)
            right_ref[MAIN * part + 48 * pair : MAIN * part + 48 * pair + 48] = both

    def right_last():
        parts = plane(HALF - 1, 0, 16)
        for part in range(2):
            right_ref[MAIN * part + 240 : MAIN * part + 256] = parts[part].astype(BF16)

    def side():
        cos, sin = plane(HALF - 1, 16, 24)
        base = jnp.concatenate([trig_ref[24:40], cos, trig_ref[48:64], sin], axis=0)
        for block, row in enumerate(FINE):
            start = 2 * MAIN + SIDE * block
            right_ref[start : start + SIDE] = (base * trig_ref[row : row + 1]).astype(BF16)

    steps = [lookup] + [functools.partial(left, pair) for pair in range(HALF)]
    return steps + [functools.partial(right, pair) for pair in range(5)] + [right_last, side]


def project_kernel(
    norm, panel_ref, wave_ref, out_ref, trig_ref, left0, left1, right0, right1, acc_ref, side_ref, power_ref
):
    lefts, rights = (left0, left1), (right0, right1)
    sources, places = panel_ref.shape[0], 2
    for right in rights:
        right[2 * MAIN + 5 * SIDE :] = jnp.zeros((256 - 5 * SIDE, right.shape[1]), BF16)
    dests = out_ref.shape[0]
    width = out_ref.shape[3]
    first, second, third = split_flat(wave_ref[...].astype(F32))
    flip0 = first > HALF - 1
    flip12 = (third > HALF - 1) | ((third == 0) & (second > HALF - 1))
    wave0 = jnp.where(flip0, EDGE - first, first)
    wave1 = jnp.where(flip12 & (second > 0), EDGE - second, second)
    wave2 = jnp.where(flip12 & (third > 0), EDGE - third, third)
    group = wave0 * 2.0 + (flip0 != flip12).astype(F32)
    side_row = (group >= SIDE_GROUPS).astype(F32) + (group >= 2 * SIDE_GROUPS).astype(F32)
    in_side = (wave2 == 0) | ((wave2 == HALF - 1) & (wave1 > 15))
    column = jnp.where(in_side, (group - SIDE_GROUPS * side_row) * 24.0, (wave2 - 1.0) * 24.0) + wave1
    group = jnp.where(in_side, 2.0 * HALF + side_row, group)
    row_iota = lax.broadcasted_iota(I32, (MAIN, width), 0).astype(F32)
    lane_iota = lax.broadcasted_iota(I32, (24, 256), 1)
    scale = 1.0 / norm

    def steps_of(chunk):
        slot = chunk % 2
        base = chunk // sources * STRIDE
        return fill_steps(panel_ref.at[chunk % sources], base, trig_ref.at[slot], lefts[slot], rights[slot])

    def powers(cc, cs, sc, ss):
        return ((cc - ss) ** 2 + (cs + sc) ** 2) * scale, ((cc + ss) ** 2 + (cs - sc) ** 2) * scale

    def square():
        for wave in range(HALF):
            start = 24 * ORDER.index(wave)
            cc, cs = acc_ref[start : start + 24, :MAIN], acc_ref[start : start + 24, MAIN:]
            sc = ss = jnp.zeros_like(cc)
            if wave:
                start = 24 * ORDER.index(11 + wave)
                sc, ss = acc_ref[start : start + 24, :MAIN], acc_ref[start : start + 24, MAIN:]
            power_ref[48 * wave : 48 * wave + 48] = jnp.concatenate(powers(cc, cs, sc, ss), axis=0).astype(BF16)

    def square_side():
        blocks = []
        for row in range(5):
            whole = side_ref[24 * row : 24 * row + 24]
            shifted = [whole] + [pltpu.roll(whole, 256 - SIDE * block, 1) for block in range(1, 5)]
            blocks.append([piece[:, :128] for piece in shifted])
        packed = [jnp.zeros((24, 256), F32) for _ in range(3)]
        for wave in range(HALF):
            coarse = (wave + 2) // 5
            fine = wave - 5 * coarse
            far, near, sign = 2 * coarse, 2 * abs(fine), 1.0 if fine > 0 else -1.0
            if not coarse:
                cos = blocks[0][max(near - 1, 0)]
                sin = blocks[0][near] if near else jnp.zeros_like(cos)
            elif not fine:
                cos, sin = blocks[far - 1][0], blocks[far][0]
            else:
                cos = blocks[far - 1][near - 1] - sign * blocks[far][near]
                sin = blocks[far][near - 1] + sign * blocks[far - 1][near]
            both = powers(cos, pltpu.roll(cos, 128 - 24, 1), sin, pltpu.roll(sin, 128 - 24, 1))
            for flipped in range(2):
                index = 2 * wave + flipped
                wide = jnp.concatenate([both[flipped], jnp.zeros((24, 128), F32)], axis=1)
                wide = jnp.where(lane_iota < 24, wide, 0.0)
                at = 24 * (index % SIDE_GROUPS)
                packed[index // SIDE_GROUPS] += pltpu.roll(wide, at, 1) if at else wide
        rows = jnp.concatenate(packed + [jnp.zeros((8, 256), F32)], axis=0)
        power_ref[576:656] = rows.astype(BF16)

    def pick(dest):
        chosen = (row_iota == column[dest : dest + 1]).astype(F32).astype(BF16)
        return jnp.dot(power_ref[...], chosen, preferred_element_type=F32)

    def store(place, dest, picked):
        total = jnp.zeros((24, width), F32)
        for g in range(2 * HALF + 3):
            total += jnp.where(group[dest : dest + 1] == g, picked[24 * g : 24 * g + 24], 0.0)
        out_ref[dest, place] = total.astype(BF16)

    chunks = places * sources
    for step in steps_of(0):
        step()
    for chunk in range(chunks):
        slot = chunk % 2
        left, right = lefts[slot], rights[slot]
        product = lax.dot_general(left[...], right[: 2 * MAIN], NT, preferred_element_type=F32)
        side = lax.dot_general(left[:128], right[2 * MAIN :], NT, preferred_element_type=F32)
        for step in steps_of(chunk + 1) if chunk + 1 < chunks else []:
            step()
        if chunk % sources == 0:
            acc_ref[...] = product
            side_ref[...] = side
        else:
            acc_ref[...] += product
            side_ref[...] += side
        if (chunk + 1) % sources == 0:
            place = chunk // sources
            square()
            square_side()
            picked = pick(0)
            for dest in range(dests):
                following = pick(dest + 1) if dest + 1 < dests else None
                store(place, dest, picked)
                picked = following


def project(panel, waves, norm):
    places, slots = 2, SLOTS
    return pl.pallas_call(
        functools.partial(project_kernel, norm),
        out_shape=jax.ShapeDtypeStruct((waves.shape[0], places, 24, waves.shape[1]), BF16),
        in_specs=[pl.BlockSpec(memory_space=pltpu.VMEM)] * 2,
        out_specs=pl.BlockSpec(memory_space=pltpu.VMEM),
        scratch_shapes=[
            pltpu.VMEM((2, 96, slots), F32),
            pltpu.VMEM((ROWS_LHS, slots), BF16),
            pltpu.VMEM((ROWS_LHS, slots), BF16),
            pltpu.VMEM((2 * MAIN + 256, slots), BF16),
            pltpu.VMEM((2 * MAIN + 256, slots), BF16),
            pltpu.VMEM((ROWS_LHS, 2 * MAIN), F32),
            pltpu.VMEM((128, 256), F32),
            pltpu.VMEM((656, MAIN), BF16),
        ],
        compiler_params=pltpu.CompilerParams(vmem_limit_bytes=48 * 2**20),
        cost_estimate=pl.CostEstimate(flops=18 * 10**9, bytes_accessed=2000000, transcendentals=0),
    )(panel, waves)


def body(modes, atom_site, site_owner, translation, wavevectors):
    col_count = lax.axis_size("col")
    sites = site_owner.shape[0]
    atoms = translation.shape[0]
    norm = 3.0 * atoms * col_count / 2.0
    message = [
        atom_site[:, 0] * 2**CELL_BITS + translation,
        wavevectors,
        jnp.pad(site_owner, (0, 128 - sites)),
    ]
    packed = jnp.concatenate(message)
    packed = jnp.broadcast_to(packed[None], (col_count, packed.shape[0]))
    meta = lax.all_to_all(packed, "col", split_axis=0, concat_axis=0, tiled=True)
    waves = meta[:, atoms : atoms + wavevectors.shape[0]]
    buckets = bucket(modes, meta, sites, atoms)
    panel = lax.all_to_all(buckets, "row", split_axis=0, concat_axis=0, tiled=True)
    power = project(panel, waves, norm)
    arrived = lax.all_to_all(power, "col", split_axis=0, concat_axis=0, tiled=True)
    arrived = arrived.transpose(1, 0, 2, 3).reshape(2, 3, -1, wavevectors.shape[0])
    projected = jnp.sum(arrived.astype(F32), axis=1)
    local = jnp.sum(projected, axis=0).reshape(lax.axis_size("row"), -1, wavevectors.shape[0])
    shares = lax.all_to_all(local, "row", split_axis=0, concat_axis=0, tiled=True)
    return projected, jnp.sum(shares, axis=0) * (1.0 / sites)


def solution(mesh):
    placed = (P("col", "row"), P(("row", "col"), None), P(), P(("row", "col")), P("col"))
    return jax.shard_map(
        body,
        mesh=mesh,
        in_specs=placed,
        out_specs=(P("row", None, "col"), P("row", "col")),
        check_vma=False,
    )
```

time: 94.6 us -> 88.6 us (0.937)
  Pallas kernels: 30.3 us -> 26.7 us
  waiting for transfers between devices: 19.5 us -> 17.7 us
    pallas_call x1, Pallas kernels: 25.9 us -> 22.7 us  [project(): pl.pallas_call(functools.partial(project_kernel, norm), out_shape=jax.Sha...]
    all_to_all x1, waiting for transfers between devices: 15.1 us -> 13.3 us  [body(): lax.all_to_all(buckets, 'row', split_axis=0, concat_axis=0, tiled=True)]
where the time goes in v3:
time: 88.6 us; the launch traced here: 88.2 us
  Pallas kernels  26.7 us (30%)
  blocking collectives  25.7 us (29%)
  waiting for transfers between devices  17.7 us (20%)
  starting transfers between devices  12.8 us (14%)
  other arithmetic  2.88 us (3%)
  local copies, waits for them, and re-layouts  1.76 us (2%)
    pallas_call x1, Pallas kernels, project(): pl.pallas_call(functools.partial(project_kernel, norm), out_shape=jax.Sha...  22.7 us
    all_to_all x1, blocking collectives, body(): lax.all_to_all(packed, 'col', split_axis=0, concat_axis=0, tiled=True)  13.9 us
    all_to_all x1, waiting for transfers between devices, body(): lax.all_to_all(buckets, 'row', split_axis=0, concat_axis=0, tiled=True)  13.3 us
    all_to_all x1, blocking collectives, body(): lax.all_to_all(power, 'col', split_axis=0, concat_axis=0, tiled=True)  11.8 us
    all_to_all x1, starting transfers between devices, body(): lax.all_to_all(buckets, 'row', split_axis=0, concat_axis=0, tiled=True)  7.43 us
    all_to_all x1, starting transfers between devices, body(): lax.all_to_all(local, 'row', split_axis=0, concat_axis=0, tiled=True)  5.34 us
    all_to_all x1, waiting for transfers between devices, body(): lax.all_to_all(local, 'row', split_axis=0, concat_axis=0, tiled=True)  4.39 us
    pallas_call x1, Pallas kernels, bucket(): pl.pallas_call(functools.partial(bucket_kernel, sites, block), out_shape=...  3.94 us
  transfers between devices with their start and end apart: 2, of which 2 were waited for; matrix products, arithmetic and copies ran while one was open for 1% of the time, Pallas kernels for 0%

profile of v3, /device:TPU:1, one launch (start us, length us, event | category | flops | bytes accessed | tf_op | source)
XLA Modules:
  0.0 88.2 jit_solution(9243832357735166258)
XLA Ops:
  0.6 0.0 copy-start.1
  0.6 0.7 broadcast_multiply_fusion.1
  1.3 0.0 copy-done.1
  1.3 0.0 copy-start.2
  1.3 0.0 copy-start.3
  1.4 0.7 copy-done.2
  2.0 0.0 copy-done.3
  2.1 13.9 %all_to_all.23 = s32[16,1,896]{2,1,0:T(1,128)S(1)} all-to-all(s32[16,1,896]{2,1,0:T(1,128)S(1)} %broadcast_in_dim.2), channel_id=1, replica_groups=mesh['row'=8,'col'=16] {'col'}, dimensions={0} | all-to-all | bytes 114688 | tf_op jit(solution)/shard_map/all_to_all | solution.py:339
  15.9 0.0 copy-start
  15.9 1.0 %copy-done = bf16[24,8192]{1,0:T(8,128)(2,1)S(1)} copy-done((bf16[24,8192]{1,0:T(8,128)(2,1)S(1)}, bf16[24,8192]{1,0:T(8,128)(2,1)}, u32[]{:S(2)}) %copy-start) | copy-done | bytes 393240
  16.9 3.9 %shard_map.68 = bf16[8,8,6912]{2,1,0:T(8,128)(2,1)} custom-call(bf16[24,8192]{1,0:T(8,128)(2,1)S(1)} %copy-done, s32[16,896]{1,0:T(8,128)S(1)} %bitcast.9), custom_call_target="tpu_custom_call" | custom-call | flops 4000000000 | bytes 1500000 | tf_op jit(solution)/shard_map/pallas_call | solution.py:120
  20.9 7.4 %all-to-all-start.1 = ((bf16[8,8,6912]{2,1,0:T(8,128)(2,1)}), bf16[8,8,6912]{2,1,0:T(8,128)(2,1)S(1)}, u32[]{:S(2)}, u32[]{:S(2)}) async-start(bf16[8,8,6912]{2,1,0:T(8,128)(2,1)} %shard_map.68), calls=%async_computation.1 | async-start | bytes 1769472 | tf_op jit(solution)/shard_map/all_to_all | solution.py:342
  28.3 13.3 %all-to-all-done.1.panel_ref = bf16[8,8,6912]{2,1,0:T(8,128)(2,1)S(1)} async-done(((bf16[8,8,6912]{2,1,0:T(8,128)(2,1)}), bf16[8,8,6912]{2,1,0:T(8,128)(2,1)S(1)}, u32[]{:S(2)}, u32[]{:S(2)}) %all-to-all-start.1) | async-done | bytes 884768 | tf_op jit(solution)/shard_map/all_to_all | solution.py:342
  41.7 22.7 %shard_map.69 = bf16[16,2,24,256]{3,2,1,0:T(8,128)(2,1)S(1)} custom-call(bf16[8,8,6912]{2,1,0:T(8,128)(2,1)S(1)} %all-to-all-done.1.panel_ref, s32[16,256]{1,0:T(8,128)S(1)} %slice.4.wave_ref), custom_call_target="tpu_custom_call" | custom-call | flops 17999998976 | bytes 2000000 | tf_op jit(solution)/shard_map/pallas_call | solution.py:307
  64.4 11.8 %all_to_all.24 = bf16[16,2,24,256]{3,2,1,0:T(8,128)(2,1)S(1)} all-to-all(bf16[16,2,24,256]{3,2,1,0:T(8,128)(2,1)S(1)} %shard_map.69), channel_id=1, replica_groups=mesh['row'=8,'col'=16] {'col'}, dimensions={0} | all-to-all | bytes 786432 | tf_op jit(solution)/shard_map/all_to_all | solution.py:344
  76.2 0.1 convert_reduce_fusion
  76.3 0.7 reduce_sum.37
  77.0 5.3 %all-to-all-start.3 = ((f32[8,16,256]{2,1,0:T(8,128)}), f32[8,16,256]{2,1,0:T(8,128)S(1)}, u32[]{:S(2)}, u32[]{:S(2)}) async-start(f32[8,16,256]{2,1,0:T(8,128)} %bitcast.4), calls=%async_computation.3 | async-start | bytes 262144 | tf_op jit(solution)/shard_map/all_to_all | solution.py:348
  82.3 0.1 convert_bitcast_fusion
  82.4 0.1 copy.9
  82.4 0.8 reduce_sum.34
  83.2 4.4 %all-to-all-done.3 = f32[8,16,256]{2,1,0:T(8,128)S(1)} async-done(((f32[8,16,256]{2,1,0:T(8,128)}), f32[8,16,256]{2,1,0:T(8,128)S(1)}, u32[]{:S(2)}, u32[]{:S(2)}) %all-to-all-start.3) | async-done | bytes 131104 | tf_op jit(solution)/shard_map/all_to_all | solution.py:348
  87.6 0.6 broadcast_multiply_fusion
  (6 shorter events, 0.1 us)
Async XLA Ops:
  0.6 0.7 copy-start.1
  1.3 0.7 copy-start.2
  1.3 0.7 copy-start.3
  15.9 1.0 %copy-start = (bf16[24,8192]{1,0:T(8,128)(2,1)S(1)}, bf16[24,8192]{1,0:T(8,128)(2,1)}, u32[]{:S(2)}) copy-start(bf16[24,8192]{1,0:T(8,128)(2,1)} %modes_hbm.1) | copy-start | bytes 1179652
  20.9 20.8 %all-to-all-start.1 = ((bf16[8,8,6912]{2,1,0:T(8,128)(2,1)}), bf16[8,8,6912]{2,1,0:T(8,128)(2,1)S(1)}, u32[]{:S(2)}, u32[]{:S(2)}) async-start(bf16[8,8,6912]{2,1,0:T(8,128)(2,1)} %shard_map.68), calls=%async_computation.1 | async-start | bytes 1769472 | tf_op jit(solution)/shard_map/all_to_all | solution.py:342
  77.0 10.6 %all-to-all-start.3 = ((f32[8,16,256]{2,1,0:T(8,128)}), f32[8,16,256]{2,1,0:T(8,128)S(1)}, u32[]{:S(2)}, u32[]{:S(2)}) async-start(f32[8,16,256]{2,1,0:T(8,128)} %bitcast.4), calls=%async_computation.3 | async-start | bytes 262144 | tf_op jit(solution)/shard_map/all_to_all | solution.py:348

commit v4 on v3

--- a/solution.py
+++ b/solution.py
@@ -16,7 +16,7 @@
 PANEL = 32
 SLOTS = 1024
 STRIDE = 3 * SLOTS + 3 * SLOTS // 8
-GROUP = 2048
+CAPACITY = 64
 ROWS_LHS = 560
 MAIN = 256
 SIDE = 48
@@ -34,26 +34,24 @@
     return first, second, rest - second * EDGE
 
 
-def sine_terms():
-    nodes = 0.25 * np.cos(np.pi * (np.arange(400) + 0.5) / 800.0)
-    turn = 2.0 * nodes
-    return [float(c) for c in np.polyfit(turn**2, np.sin(2.0 * np.pi * turn) / turn, 6)]
-
-
-SINE = sine_terms()
-
-
-def sine(turn):
-    square = turn * turn
-    total = SINE[0]
-    for term in SINE[1:]:
+def turn_terms(function, odd, count):
+    turn = 0.5 * np.cos(np.pi * (np.arange(400) + 0.5) / 800.0)
+    values = function(2.0 * np.pi * turn) / (turn if odd else 1.0)
+    return [float(c) for c in np.polyfit(turn**2, values, count - 1)]
+
+
+SINE = turn_terms(np.sin, True, 6)
+COSINE = turn_terms(np.cos, False, 7)
+
+
+def horner(terms, square):
+    total = terms[0]
+    for term in terms[1:]:
         total = total * square + term
-    return total * turn
-
-
-def bucket_kernel(sites, block, modes_hbm, meta_ref, out_ref, modes_ref, cell_ref, copied):
-    copy = pltpu.make_async_copy(modes_hbm, modes_ref, copied)
-    copy.start()
+    return total
+
+
+def bucket_kernel(sites, block, modes_ref, meta_ref, out_ref, cell_ref):
     blocks = meta_ref.shape[0]
     owner_row = meta_ref[0:1, meta_ref.shape[1] - 128 :][:, :sites]
     down = lax.broadcasted_iota(I32, (sites, sites), 0)
@@ -70,70 +68,67 @@
     target = lax.broadcasted_iota(I32, (block, block), 1)
     earlier = (source < target).astype(F32).astype(BF16)
     before = jnp.dot(stacked, earlier, preferred_element_type=F32)
-    per_group = GROUP // block
-    upper = lax.broadcasted_iota(I32, (sites * blocks, sites * blocks), 0)
-    lower = lax.broadcasted_iota(I32, (sites * blocks, sites * blocks), 1)
-    same = (upper // per_group == lower // per_group) & (lower < upper)
-    offsets = jnp.sum(
-        jnp.dot(same.astype(F32).astype(BF16), stacked, preferred_element_type=F32), axis=1, keepdims=True
-    )
-    before = before + offsets
     rank = jnp.zeros(meta.shape, F32)
     place = jnp.zeros(meta.shape, F32)
     for s in range(sites):
         rank += hot[s] * before[s * blocks : (s + 1) * blocks]
         place += hot[s] * order[s : s + 1]
-    copy.wait()
-    slots = GROUP // 8
+    quarter = jnp.floor(place * 0.25)
+    column = (place - 4.0 * quarter) * CAPACITY + rank
+    slots = 4 * CAPACITY
     slot_iota = lax.broadcasted_iota(I32, (slots, block), 0).astype(F32)
+    low_lanes = lax.broadcasted_iota(I32, (PANEL, 128), 1) < CAPACITY
     pad = jnp.zeros((5, block), F32)
-    for group in range(blocks // per_group):
-        total = None
-        for part in range(per_group):
-            b = group * per_group + part
-            rows = [c[b : b + 1] for c in coords]
-            panel = jnp.concatenate([modes_ref[:, b * block : (b + 1) * block].astype(F32), *rows, pad], axis=0)
-            place_row = place[b : b + 1]
-            left = jnp.concatenate(
-                [jnp.where(place_row == p, panel, 0.0).astype(BF16) for p in range(sites)], axis=0
-            )
-            right = (slot_iota == rank[b : b + 1]).astype(F32).astype(BF16)
-            product = lax.dot_general(left, right, NT, preferred_element_type=F32)
-            total = product if total is None else total + product
+
+    def sort_block(b):
+        rows = [c[b : b + 1] for c in coords]
+        panel = jnp.concatenate([modes_ref[:, b * block : (b + 1) * block].astype(F32), *rows, pad], axis=0)
+        row = quarter[b : b + 1]
+        left = jnp.concatenate([jnp.where(row == q, panel, 0.0).astype(BF16) for q in range(sites // 4)], axis=0)
+        right = (slot_iota == column[b : b + 1]).astype(F32).astype(BF16)
+        return lax.dot_general(left, right, NT, preferred_element_type=F32)
+
+    for pair in range(blocks // 2):
+        even, odd = sort_block(2 * pair), sort_block(2 * pair + 1)
         for p in range(sites):
-            start = (p % 2) * STRIDE + group * slots
+            rows = slice((p // 4) * PANEL, (p // 4) * PANEL + PANEL)
+            lanes = slice((p % 4) // 2 * 128, (p % 4) // 2 * 128 + 128)
+            low, high = even[rows, lanes], odd[rows, lanes]
+            if p % 2:
+                low = pltpu.roll(low, CAPACITY, 1)
+            else:
+                high = pltpu.roll(high, CAPACITY, 1)
+            total = jnp.where(low_lanes, low, high)
+            start = (p % 2) * STRIDE + 128 * pair
             for part in range(3):
-                piece = total[p * PANEL + 8 * part : p * PANEL + 8 * part + 8].astype(BF16)
-                out_ref[p // 2, :, start + part * SLOTS : start + part * SLOTS + slots] = piece
-            for half in range(slots // 128):
-                row = group * (slots // 128) + half
-                for axis in range(3):
-                    line = total[p * PANEL + 24 + axis : p * PANEL + 25 + axis, 128 * half : 128 * half + 128]
-                    cell_ref[p, row : row + 1, 128 * axis : 128 * axis + 128] = line
+                piece = total[8 * part : 8 * part + 8].astype(BF16)
+                out_ref[p // 2, :, start + part * SLOTS : start + part * SLOTS + 128] = piece
+            for axis in range(3):
+                cell_ref[p, pair : pair + 1, 128 * axis : 128 * axis + 128] = total[24 + axis : 25 + axis]
     for p in range(sites):
         start = (p % 2) * STRIDE + 3 * SLOTS
         out_ref[p // 2, :, start : start + 384] = cell_ref[p].astype(BF16)
 
 
 def bucket(modes, meta, sites, block):
-    rows, atoms = modes.shape
     return pl.pallas_call(
         functools.partial(bucket_kernel, sites, block),
         out_shape=jax.ShapeDtypeStruct((sites // 2, 8, 2 * STRIDE), BF16),
-        in_specs=[pl.BlockSpec(memory_space=pl.ANY), pl.BlockSpec(memory_space=pltpu.VMEM)],
+        in_specs=[pl.BlockSpec(memory_space=pltpu.VMEM)] * 2,
         out_specs=pl.BlockSpec(memory_space=pltpu.VMEM),
-        scratch_shapes=[
-            pltpu.VMEM((rows, atoms), BF16),
-            pltpu.VMEM((sites, 8, 384), F32),
-            pltpu.SemaphoreType.DMA(()),
-        ],
+        scratch_shapes=[pltpu.VMEM((sites, 8, 384), F32)],
         compiler_params=pltpu.CompilerParams(vmem_limit_bytes=48 * 2**20),
         cost_estimate=pl.CostEstimate(flops=4 * 10**9, bytes_accessed=1500000, transcendentals=0),
     )(modes, meta)
 
 
+def table_row(row):
+    return row if row < HALF else row + 1
+
+
 def fill_steps(panel_ref, base, trig_ref, left_ref, right_ref):
     width = SLOTS
+    loaded = []
 
     def lookup():
         lines = panel_ref[:, base + 3 * SLOTS : base + STRIDE].astype(F32)
@@ -142,25 +137,26 @@
             for axis in range(3)
         ]
         rows = lax.broadcasted_iota(I32, (24, width), 0).astype(F32)
-        waves = [
-            (jnp.where(rows < HALF, rows, rows - 11.0), jnp.where(rows < HALF, 0.25, 0.0)),
-            (rows, 0.25),
-            (rows, 0.0),
-            (jnp.where(rows < HALF, rows, rows - 12.0), jnp.where(rows < HALF, 0.25, 0.0)),
-        ]
-        for part, axis in enumerate((0, 1, 1, 2)):
-            wave, shift = waves[part]
-            turn = wave * (cells[axis] * (1.0 / EDGE)) + shift
-            trig_ref[24 * part : 24 * part + 24] = sine(turn - jnp.round(turn))
+        starts = ((0, 12, 16), (24, 48, 24), (72, 88, 16))
+        for axis, (cos_start, sin_start, count) in enumerate(starts):
+            turn = rows[:count] * (cells[axis] * (1.0 / EDGE))
+            turn = turn - jnp.round(turn)
+            square = turn * turn
+            cos, sin = horner(COSINE, square), horner(SINE, square) * turn
+            if axis == 0:
+                cos, sin = cos[:HALF], sin[:HALF]
+            trig_ref[cos_start : cos_start + cos.shape[0]] = cos
+            trig_ref[sin_start : sin_start + sin.shape[0]] = sin
 
     def left(pair):
-        values = jnp.concatenate(
-            [panel_ref[:, base + SLOTS * part : base + SLOTS * part + SLOTS].astype(F32) for part in range(3)], axis=0
-        )
-        row = ORDER[2 * pair]
+        if not loaded:
+            parts = [panel_ref[:, base + SLOTS * part : base + SLOTS * part + SLOTS] for part in range(3)]
+            loaded.append(jnp.concatenate([part.astype(F32) for part in parts], axis=0))
+        values = loaded[0]
+        row = table_row(ORDER[2 * pair])
         first = values * trig_ref[row : row + 1]
         if pair < HALF - 1:
-            row = ORDER[2 * pair + 1]
+            row = table_row(ORDER[2 * pair + 1])
             second = values * trig_ref[row : row + 1]
         else:
             second = jnp.zeros((8, width), F32)
@@ -169,7 +165,7 @@
 
     def plane(wave, low, high):
         cos1, sin1 = trig_ref[24 + low : 24 + high], trig_ref[48 + low : 48 + high]
-        cos2, sin2 = trig_ref[72 + wave : 73 + wave], trig_ref[84 + wave : 85 + wave]
+        cos2, sin2 = trig_ref[72 + wave : 73 + wave], trig_ref[88 + wave : 89 + wave]
         return cos1 * cos2 - sin1 * sin2, sin1 * cos2 + cos1 * sin2
 
     def right(pair):
@@ -186,7 +182,7 @@
     def side():
         cos, sin = plane(HALF - 1, 16, 24)
         base = jnp.concatenate([trig_ref[24:40], cos, trig_ref[48:64], sin], axis=0)
-        for block, row in enumerate(FINE):
+        for block, row in enumerate(map(table_row, FINE)):
             start = 2 * MAIN + SIDE * block
             right_ref[start : start + SIDE] = (base * trig_ref[row : row + 1]).astype(BF16)
 
@@ -226,20 +222,20 @@
     def powers(cc, cs, sc, ss):
         return ((cc - ss) ** 2 + (cs + sc) ** 2) * scale, ((cc + ss) ** 2 + (cs - sc) ** 2) * scale
 
-    def square():
+    def square(place):
         for wave in range(HALF):
             start = 24 * ORDER.index(wave)
-            cc, cs = acc_ref[start : start + 24, :MAIN], acc_ref[start : start + 24, MAIN:]
+            cc, cs = acc_ref[place, start : start + 24, :MAIN], acc_ref[place, start : start + 24, MAIN:]
             sc = ss = jnp.zeros_like(cc)
             if wave:
                 start = 24 * ORDER.index(11 + wave)
-                sc, ss = acc_ref[start : start + 24, :MAIN], acc_ref[start : start + 24, MAIN:]
+                sc, ss = acc_ref[place, start : start + 24, :MAIN], acc_ref[place, start : start + 24, MAIN:]
             power_ref[48 * wave : 48 * wave + 48] = jnp.concatenate(powers(cc, cs, sc, ss), axis=0).astype(BF16)
 
-    def square_side():
+    def square_side(place):
         blocks = []
         for row in range(5):
-            whole = side_ref[24 * row : 24 * row + 24]
+            whole = side_ref[place, 24 * row : 24 * row + 24]
             shifted = [whole] + [pltpu.roll(whole, 256 - SIDE * block, 1) for block in range(1, 5)]
             blocks.append([piece[:, :128] for piece in shifted])
         packed = [jnp.zeros((24, 256), F32) for _ in range(3)]
@@ -275,6 +271,15 @@
             total += jnp.where(group[dest : dest + 1] == g, picked[24 * g : 24 * g + 24], 0.0)
         out_ref[dest, place] = total.astype(BF16)
 
+    def finish(place):
+        square(place)
+        square_side(place)
+        picked = pick(0)
+        for dest in range(dests):
+            following = pick(dest + 1) if dest + 1 < dests else None
+            store(place, dest, picked)
+            picked = following
+
     chunks = places * sources
     for step in steps_of(0):
         step()
@@ -285,21 +290,15 @@
         side = lax.dot_general(left[:128], right[2 * MAIN :], NT, preferred_element_type=F32)
         for step in steps_of(chunk + 1) if chunk + 1 < chunks else []:
             step()
+        place = chunk // sources
         if chunk % sources == 0:
-            acc_ref[...] = product
-            side_ref[...] = side
+            acc_ref[place] = product
+            side_ref[place] = side
         else:
-            acc_ref[...] += product
-            side_ref[...] += side
+            acc_ref[place] += product
+            side_ref[place] += side
         if (chunk + 1) % sources == 0:
-            place = chunk // sources
-            square()
-            square_side()
-            picked = pick(0)
-            for dest in range(dests):
-                following = pick(dest + 1) if dest + 1 < dests else None
-                store(place, dest, picked)
-                picked = following
+            finish(place)
 
 
 def project(panel, waves, norm):
@@ -310,13 +309,13 @@
         in_specs=[pl.BlockSpec(memory_space=pltpu.VMEM)] * 2,
         out_specs=pl.BlockSpec(memory_space=pltpu.VMEM),
         scratch_shapes=[
-            pltpu.VMEM((2, 96, slots), F32),
+            pltpu.VMEM((2, 104, slots), F32),
             pltpu.VMEM((ROWS_LHS, slots), BF16),
             pltpu.VMEM((ROWS_LHS, slots), BF16),
             pltpu.VMEM((2 * MAIN + 256, slots), BF16),
             pltpu.VMEM((2 * MAIN + 256, slots), BF16),
-            pltpu.VMEM((ROWS_LHS, 2 * MAIN), F32),
-            pltpu.VMEM((128, 256), F32),
+            pltpu.VMEM((places, ROWS_LHS, 2 * MAIN), F32),
+            pltpu.VMEM((places, 128, 256), F32),
             pltpu.VMEM((656, MAIN), BF16),
         ],
         compiler_params=pltpu.CompilerParams(vmem_limit_bytes=48 * 2**20),

time: 88.6 us -> 87.2 us (0.984)
  Pallas kernels: 26.7 us -> 25.3 us
    pallas_call x1, Pallas kernels: 3.94 us -> 2.92 us  [bucket(): pl.pallas_call(functools.partial(bucket_kernel, sites, block), out_shape=...]
where the time goes in v4:
time: 87.2 us; the launch traced here: 86.8 us
  blocking collectives  25.7 us (29%)
  Pallas kernels  25.3 us (29%)
  waiting for transfers between devices  17.7 us (20%)
  starting transfers between devices  12.8 us (15%)
  other arithmetic  2.88 us (3%)
  local copies, waits for them, and re-layouts  1.76 us (2%)
    pallas_call x1, Pallas kernels, project(): pl.pallas_call(functools.partial(project_kernel, norm), out_shape=jax.Sha...  22.3 us
    all_to_all x1, blocking collectives, body(): lax.all_to_all(packed, 'col', split_axis=0, concat_axis=0, tiled=True)  13.9 us
    all_to_all x1, waiting for transfers between devices, body(): lax.all_to_all(buckets, 'row', split_axis=0, concat_axis=0, tiled=True)  13.3 us
    all_to_all x1, blocking collectives, body(): lax.all_to_all(power, 'col', split_axis=0, concat_axis=0, tiled=True)  11.8 us
    all_to_all x1, starting transfers between devices, body(): lax.all_to_all(buckets, 'row', split_axis=0, concat_axis=0, tiled=True)  7.41 us
    all_to_all x1, starting transfers between devices, body(): lax.all_to_all(local, 'row', split_axis=0, concat_axis=0, tiled=True)  5.35 us
    all_to_all x1, waiting for transfers between devices, body(): lax.all_to_all(local, 'row', split_axis=0, concat_axis=0, tiled=True)  4.39 us
    pallas_call x1, Pallas kernels, bucket(): pl.pallas_call(functools.partial(bucket_kernel, sites, block), out_shape=...  2.92 us
  transfers between devices with their start and end apart: 2, of which 2 were waited for; matrix products, arithmetic and copies ran while one was open for 1% of the time, Pallas kernels for 0%

profile of v4, /device:TPU:1, one launch (start us, length us, event | category | flops | bytes accessed | tf_op | source)
XLA Modules:
  0.0 86.8 jit_solution(6953399099703243645)
XLA Ops:
  0.6 0.0 copy-start.1
  0.6 0.7 broadcast_multiply_fusion.1
  1.3 0.0 copy-done.1
  1.3 0.0 copy-start.2
  1.3 0.0 copy-start.3
  1.4 0.7 copy-done.2
  2.0 0.0 copy-done.3
  2.1 13.9 %all_to_all.23 = s32[16,1,896]{2,1,0:T(1,128)S(1)} all-to-all(s32[16,1,896]{2,1,0:T(1,128)S(1)} %broadcast_in_dim.2), channel_id=1, replica_groups=mesh['row'=8,'col'=16] {'col'}, dimensions={0} | all-to-all | bytes 114688 | tf_op jit(solution)/shard_map/all_to_all | solution.py:338
  15.9 0.0 copy-start
  15.9 1.0 %copy-done = bf16[24,8192]{1,0:T(8,128)(2,1)S(1)} copy-done((bf16[24,8192]{1,0:T(8,128)(2,1)S(1)}, bf16[24,8192]{1,0:T(8,128)(2,1)}, u32[]{:S(2)}) %copy-start) | copy-done | bytes 393240
  16.9 2.9 %shard_map.68 = bf16[8,8,6912]{2,1,0:T(8,128)(2,1)} custom-call(bf16[24,8192]{1,0:T(8,128)(2,1)S(1)} %copy-done, s32[16,896]{1,0:T(8,128)S(1)} %bitcast.9), custom_call_target="tpu_custom_call" | custom-call | flops 4000000000 | bytes 1500000 | tf_op jit(solution)/shard_map/pallas_call | solution.py:114
  19.9 7.4 %all-to-all-start.1 = ((bf16[8,8,6912]{2,1,0:T(8,128)(2,1)}), bf16[8,8,6912]{2,1,0:T(8,128)(2,1)S(1)}, u32[]{:S(2)}, u32[]{:S(2)}) async-start(bf16[8,8,6912]{2,1,0:T(8,128)(2,1)} %shard_map.68), calls=%async_computation.1 | async-start | bytes 1769472 | tf_op jit(solution)/shard_map/all_to_all | solution.py:341
  27.3 13.3 %all-to-all-done.1.panel_ref = bf16[8,8,6912]{2,1,0:T(8,128)(2,1)S(1)} async-done(((bf16[8,8,6912]{2,1,0:T(8,128)(2,1)}), bf16[8,8,6912]{2,1,0:T(8,128)(2,1)S(1)}, u32[]{:S(2)}, u32[]{:S(2)}) %all-to-all-start.1) | async-done | bytes 884768 | tf_op jit(solution)/shard_map/all_to_all | solution.py:341
  40.6 22.3 %shard_map.69 = bf16[16,2,24,256]{3,2,1,0:T(8,128)(2,1)S(1)} custom-call(bf16[8,8,6912]{2,1,0:T(8,128)(2,1)S(1)} %all-to-all-done.1.panel_ref, s32[16,256]{1,0:T(8,128)S(1)} %slice.4.wave_ref), custom_call_target="tpu_custom_call" | custom-call | flops 17999998976 | bytes 2000000 | tf_op jit(solution)/shard_map/pallas_call | solution.py:306
  63.0 11.8 %all_to_all.24 = bf16[16,2,24,256]{3,2,1,0:T(8,128)(2,1)S(1)} all-to-all(bf16[16,2,24,256]{3,2,1,0:T(8,128)(2,1)S(1)} %shard_map.69), channel_id=1, replica_groups=mesh['row'=8,'col'=16] {'col'}, dimensions={0} | all-to-all | bytes 786432 | tf_op jit(solution)/shard_map/all_to_all | solution.py:343
  74.8 0.1 convert_reduce_fusion
  74.8 0.7 reduce_sum.37
  75.5 5.3 %all-to-all-start.3 = ((f32[8,16,256]{2,1,0:T(8,128)}), f32[8,16,256]{2,1,0:T(8,128)S(1)}, u32[]{:S(2)}, u32[]{:S(2)}) async-start(f32[8,16,256]{2,1,0:T(8,128)} %bitcast.4), calls=%async_computation.3 | async-start | bytes 262144 | tf_op jit(solution)/shard_map/all_to_all | solution.py:347
  80.9 0.1 convert_bitcast_fusion
  80.9 0.1 copy.9
  81.0 0.8 reduce_sum.34
  81.8 4.4 %all-to-all-done.3 = f32[8,16,256]{2,1,0:T(8,128)S(1)} async-done(((f32[8,16,256]{2,1,0:T(8,128)}), f32[8,16,256]{2,1,0:T(8,128)S(1)}, u32[]{:S(2)}, u32[]{:S(2)}) %all-to-all-start.3) | async-done | bytes 131104 | tf_op jit(solution)/shard_map/all_to_all | solution.py:347
  86.2 0.6 broadcast_multiply_fusion
  (6 shorter events, 0.1 us)
Async XLA Ops:
  0.6 0.7 copy-start.1
  1.3 0.7 copy-start.2
  1.3 0.7 copy-start.3
  15.9 1.0 %copy-start = (bf16[24,8192]{1,0:T(8,128)(2,1)S(1)}, bf16[24,8192]{1,0:T(8,128)(2,1)}, u32[]{:S(2)}) copy-start(bf16[24,8192]{1,0:T(8,128)(2,1)} %modes_ref.1) | copy-start | bytes 1179652
  19.9 20.8 %all-to-all-start.1 = ((bf16[8,8,6912]{2,1,0:T(8,128)(2,1)}), bf16[8,8,6912]{2,1,0:T(8,128)(2,1)S(1)}, u32[]{:S(2)}, u32[]{:S(2)}) async-start(bf16[8,8,6912]{2,1,0:T(8,128)(2,1)} %shard_map.68), calls=%async_computation.1 | async-start | bytes 1769472 | tf_op jit(solution)/shard_map/all_to_all | solution.py:341
  75.5 10.6 %all-to-all-start.3 = ((f32[8,16,256]{2,1,0:T(8,128)}), f32[8,16,256]{2,1,0:T(8,128)S(1)}, u32[]{:S(2)}, u32[]{:S(2)}) async-start(f32[8,16,256]{2,1,0:T(8,128)} %bitcast.4), calls=%async_computation.3 | async-start | bytes 262144 | tf_op jit(solution)/shard_map/all_to_all | solution.py:347

commit v5 on v4

--- a/solution.py
+++ b/solution.py
@@ -51,7 +51,7 @@
     return total
 
 
-def bucket_kernel(sites, block, modes_ref, meta_ref, out_ref, cell_ref):
+def rank_kernel(sites, block, meta_ref, plan_ref):
     blocks = meta_ref.shape[0]
     owner_row = meta_ref[0:1, meta_ref.shape[1] - 128 :][:, :sites]
     down = lax.broadcasted_iota(I32, (sites, sites), 0)
@@ -75,17 +75,24 @@
         place += hot[s] * order[s : s + 1]
     quarter = jnp.floor(place * 0.25)
     column = (place - 4.0 * quarter) * CAPACITY + rank
+    for row, values in enumerate((quarter, column, *coords)):
+        plan_ref[row] = values
+
+
+def bucket_kernel(modes_ref, plan_ref, out_ref, cell_ref):
+    sites = cell_ref.shape[0]
+    blocks, block = plan_ref.shape[1:]
     slots = 4 * CAPACITY
     slot_iota = lax.broadcasted_iota(I32, (slots, block), 0).astype(F32)
     low_lanes = lax.broadcasted_iota(I32, (PANEL, 128), 1) < CAPACITY
     pad = jnp.zeros((5, block), F32)
 
     def sort_block(b):
-        rows = [c[b : b + 1] for c in coords]
+        rows = [plan_ref[axis, b : b + 1] for axis in (2, 3, 4)]
         panel = jnp.concatenate([modes_ref[:, b * block : (b + 1) * block].astype(F32), *rows, pad], axis=0)
-        row = quarter[b : b + 1]
+        row = plan_ref[0, b : b + 1]
         left = jnp.concatenate([jnp.where(row == q, panel, 0.0).astype(BF16) for q in range(sites // 4)], axis=0)
-        right = (slot_iota == column[b : b + 1]).astype(F32).astype(BF16)
+        right = (slot_iota == plan_ref[1, b : b + 1]).astype(F32).astype(BF16)
         return lax.dot_general(left, right, NT, preferred_element_type=F32)
 
     for pair in range(blocks // 2):
@@ -111,15 +118,23 @@
 
 
 def bucket(modes, meta, sites, block):
+    plan = pl.pallas_call(
+        functools.partial(rank_kernel, sites, block),
+        out_shape=jax.ShapeDtypeStruct((5, meta.shape[0], block), F32),
+        in_specs=[pl.BlockSpec(memory_space=pltpu.VMEM)],
+        out_specs=pl.BlockSpec(memory_space=pltpu.VMEM),
+        compiler_params=pltpu.CompilerParams(vmem_limit_bytes=16 * 2**20),
+        cost_estimate=pl.CostEstimate(flops=10**9, bytes_accessed=300000, transcendentals=0),
+    )(meta)
     return pl.pallas_call(
-        functools.partial(bucket_kernel, sites, block),
+        bucket_kernel,
         out_shape=jax.ShapeDtypeStruct((sites // 2, 8, 2 * STRIDE), BF16),
         in_specs=[pl.BlockSpec(memory_space=pltpu.VMEM)] * 2,
         out_specs=pl.BlockSpec(memory_space=pltpu.VMEM),
         scratch_shapes=[pltpu.VMEM((sites, 8, 384), F32)],
         compiler_params=pltpu.CompilerParams(vmem_limit_bytes=48 * 2**20),
         cost_estimate=pl.CostEstimate(flops=4 * 10**9, bytes_accessed=1500000, transcendentals=0),
-    )(modes, meta)
+    )(modes, plan)
 
 
 def table_row(row):

time: 87.2 us -> 86.9 us (level)
    pallas_call x1 -> x2, Pallas kernels: 2.92 us -> 2.95 us  [the longest x1 2.64 us: bucket(): pl.pallas_call(bucket_kernel, out_shape=jax.ShapeDtypeStruct((sites // 2,...]
where the time goes in v5:
time: 86.9 us; the launch traced here: 86.5 us
  blocking collectives  25.7 us (30%)
  Pallas kernels  25.3 us (29%)
  waiting for transfers between devices  17.7 us (20%)
  starting transfers between devices  12.8 us (15%)
  other arithmetic  2.88 us (3%)
  local copies, waits for them, and re-layouts  1.44 us (2%)
    pallas_call x1, Pallas kernels, project(): pl.pallas_call(functools.partial(project_kernel, norm), out_shape=jax.Sha...  22.3 us
    all_to_all x1, blocking collectives, body(): lax.all_to_all(packed, 'col', split_axis=0, concat_axis=0, tiled=True)  13.9 us
    all_to_all x1, waiting for transfers between devices, body(): lax.all_to_all(buckets, 'row', split_axis=0, concat_axis=0, tiled=True)  13.3 us
    all_to_all x1, blocking collectives, body(): lax.all_to_all(power, 'col', split_axis=0, concat_axis=0, tiled=True)  11.8 us
    all_to_all x1, starting transfers between devices, body(): lax.all_to_all(buckets, 'row', split_axis=0, concat_axis=0, tiled=True)  7.41 us
    all_to_all x1, starting transfers between devices, body(): lax.all_to_all(local, 'row', split_axis=0, concat_axis=0, tiled=True)  5.35 us
    all_to_all x1, waiting for transfers between devices, body(): lax.all_to_all(local, 'row', split_axis=0, concat_axis=0, tiled=True)  4.39 us
    pallas_call x1, Pallas kernels, bucket(): pl.pallas_call(bucket_kernel, out_shape=jax.ShapeDtypeStruct((sites // 2,...  2.64 us
  transfers between devices with their start and end apart: 2, of which 2 were waited for; matrix products, arithmetic and copies ran while one was open for 1% of the time, Pallas kernels for 0%

profile of v5, /device:TPU:1, one launch (start us, length us, event | category | flops | bytes accessed | tf_op | source)
XLA Modules:
  0.0 86.5 jit_solution(4228376188819223368)
XLA Ops:
  0.6 0.0 copy-start.1
  0.6 0.7 broadcast_multiply_fusion.1
  1.3 0.0 copy-done.1
  1.3 0.0 copy-start.2
  1.3 0.0 copy-start.3
  1.4 0.7 copy-done.2
  2.0 0.0 copy-done.3
  2.1 13.9 %all_to_all.23 = s32[16,1,896]{2,1,0:T(1,128)S(1)} all-to-all(s32[16,1,896]{2,1,0:T(1,128)S(1)} %broadcast_in_dim.2), channel_id=1, replica_groups=mesh['row'=8,'col'=16] {'col'}, dimensions={0} | all-to-all | bytes 114688 | tf_op jit(solution)/shard_map/all_to_all | solution.py:353
  15.9 0.0 copy-start
  15.9 0.3 shard_map.68.plan_ref
  16.3 0.7 copy-done
  16.9 2.6 %shard_map.69 = bf16[8,8,6912]{2,1,0:T(8,128)(2,1)} custom-call(bf16[24,8192]{1,0:T(8,128)(2,1)S(1)} %copy-done, f32[5,16,512]{2,1,0:T(8,128)S(1)} %shard_map.68.plan_ref), custom_call_target="tpu_custom_call" | custom-call | flops 4000000000 | bytes 1500000 | tf_op jit(solution)/shard_map/pallas_call | solution.py:129
  19.6 7.4 %all-to-all-start.1 = ((bf16[8,8,6912]{2,1,0:T(8,128)(2,1)}), bf16[8,8,6912]{2,1,0:T(8,128)(2,1)S(1)}, u32[]{:S(2)}, u32[]{:S(2)}) async-start(bf16[8,8,6912]{2,1,0:T(8,128)(2,1)} %shard_map.69), calls=%async_computation.1 | async-start | bytes 1769472 | tf_op jit(solution)/shard_map/all_to_all | solution.py:356
  27.0 13.3 %all-to-all-done.1.panel_ref = bf16[8,8,6912]{2,1,0:T(8,128)(2,1)S(1)} async-done(((bf16[8,8,6912]{2,1,0:T(8,128)(2,1)}), bf16[8,8,6912]{2,1,0:T(8,128)(2,1)S(1)}, u32[]{:S(2)}, u32[]{:S(2)}) %all-to-all-start.1) | async-done | bytes 884768 | tf_op jit(solution)/shard_map/all_to_all | solution.py:356
  40.3 22.3 %shard_map.70 = bf16[16,2,24,256]{3,2,1,0:T(8,128)(2,1)S(1)} custom-call(bf16[8,8,6912]{2,1,0:T(8,128)(2,1)S(1)} %all-to-all-done.1.panel_ref, s32[16,256]{1,0:T(8,128)S(1)} %slice.4.wave_ref), custom_call_target="tpu_custom_call" | custom-call | flops 17999998976 | bytes 2000000 | tf_op jit(solution)/shard_map/pallas_call | solution.py:321
  62.7 11.8 %all_to_all.24 = bf16[16,2,24,256]{3,2,1,0:T(8,128)(2,1)S(1)} all-to-all(bf16[16,2,24,256]{3,2,1,0:T(8,128)(2,1)S(1)} %shard_map.70), channel_id=1, replica_groups=mesh['row'=8,'col'=16] {'col'}, dimensions={0} | all-to-all | bytes 786432 | tf_op jit(solution)/shard_map/all_to_all | solution.py:358
  74.5 0.1 convert_reduce_fusion
  74.6 0.7 reduce_sum.37
  75.2 5.3 %all-to-all-start.3 = ((f32[8,16,256]{2,1,0:T(8,128)}), f32[8,16,256]{2,1,0:T(8,128)S(1)}, u32[]{:S(2)}, u32[]{:S(2)}) async-start(f32[8,16,256]{2,1,0:T(8,128)} %bitcast.4), calls=%async_computation.3 | async-start | bytes 262144 | tf_op jit(solution)/shard_map/all_to_all | solution.py:362
  80.6 0.1 convert_bitcast_fusion
  80.7 0.1 copy.9
  80.7 0.8 reduce_sum.34
  81.5 4.4 %all-to-all-done.3 = f32[8,16,256]{2,1,0:T(8,128)S(1)} async-done(((f32[8,16,256]{2,1,0:T(8,128)}), f32[8,16,256]{2,1,0:T(8,128)S(1)}, u32[]{:S(2)}, u32[]{:S(2)}) %all-to-all-start.3) | async-done | bytes 131104 | tf_op jit(solution)/shard_map/all_to_all | solution.py:362
  85.9 0.6 broadcast_multiply_fusion
  (6 shorter events, 0.1 us)
Async XLA Ops:
  0.6 0.7 copy-start.1
  1.3 0.7 copy-start.2
  1.3 0.7 copy-start.3
  15.9 1.0 %copy-start = (bf16[24,8192]{1,0:T(8,128)(2,1)S(1)}, bf16[24,8192]{1,0:T(8,128)(2,1)}, u32[]{:S(2)}) copy-start(bf16[24,8192]{1,0:T(8,128)(2,1)} %modes_ref.1) | copy-start | bytes 1179652
  19.6 20.8 %all-to-all-start.1 = ((bf16[8,8,6912]{2,1,0:T(8,128)(2,1)}), bf16[8,8,6912]{2,1,0:T(8,128)(2,1)S(1)}, u32[]{:S(2)}, u32[]{:S(2)}) async-start(bf16[8,8,6912]{2,1,0:T(8,128)(2,1)} %shard_map.69), calls=%async_computation.1 | async-start | bytes 1769472 | tf_op jit(solution)/shard_map/all_to_all | solution.py:356
  75.2 10.6 %all-to-all-start.3 = ((f32[8,16,256]{2,1,0:T(8,128)}), f32[8,16,256]{2,1,0:T(8,128)S(1)}, u32[]{:S(2)}, u32[]{:S(2)}) async-start(f32[8,16,256]{2,1,0:T(8,128)} %bitcast.4), calls=%async_computation.3 | async-start | bytes 262144 | tf_op jit(solution)/shard_map/all_to_all | solution.py:362
